TPU v7x, 512 devices: a whole 4x8x8 slice. The times are simulated.
512 devices in a mesh: wide: 64 (over z, y_hi, core), narrow: 8 (over y_lo, x).
Axes of the slice: x: 4, y: 8 (y_hi: 4, y_lo: 2; y = y_hi * 2 + y_lo), z: 8, core: 2. Of those that a mesh axis runs over, the one named last changes fastest.
Arguments:
- x_tokens: float32 [512, 6144], P('wide', 'narrow'), may hold values from -32 to 32
- grad_out: float32 [512, 6144], P('wide', 'narrow'), may hold values from -32 to 32
- w_in: float32 [6144, 24576], P('narrow', 'wide'), may hold values from -4 to 4
- b_in: float32 [24576], P('wide'), may hold values from -4 to 4
- w_out: float32 [24576, 6144], P('wide', 'narrow'), may hold values from -7 to 7
Outputs:
- grad_in: float32 [512, 6144], P('wide', 'narrow')
- gw_in: float32 [6144, 24576], P('narrow', 'wide')
- gw_out: float32 [24576, 6144], P('wide', 'narrow')
- gb_in: float32 [24576], P('wide')
- gb_out: float32 [6144], P('narrow')
All inputs are finite; a program needn't handle non-finite values.
Results may differ from a plain program's by a relative error of at most 0.0003.
Values sent between devices are 32-bit elements; how exact they have to be, the bound alone decides.
A program may use at most 64 MiB of HBM per device.

v0:
```python
import math

import jax
import jax.numpy as jnp
from jax import lax
from jax.sharding import PartitionSpec as P

D = 6144
FF = 24576


tanh_scale = math.sqrt(2.0 / math.pi)
cubic_weight = 0.044715


def gelu_parts(pre):
    inner = tanh_scale * (pre + cubic_weight * pre * pre * pre)
    tangent = jnp.tanh(inner)
    value = 0.5 * pre * (1.0 + tangent)
    slope = 0.5 * (1.0 + tangent) + 0.5 * pre * (1.0 - tangent * tangent) * tanh_scale * (
        1.0 + 3.0 * cubic_weight * pre * pre
    )
    return (value, slope)


def contract_first(left, right):
    return lax.dot_general(
        left,
        right,
        (((0,), (0,)), ((), ())),
        precision=lax.Precision.HIGHEST,
        preferred_element_type=jnp.float32,
    )


def contract_last(left, right):
    return lax.dot_general(
        left,
        right,
        (((1,), (1,)), ((), ())),
        precision=lax.Precision.HIGHEST,
        preferred_element_type=jnp.float32,
    )


def local(x_tokens, grad_out, w_in, b_in, w_out):
    x_piece, out_piece = lax.all_gather((x_tokens, grad_out), "wide", axis=0, tiled=True)
    pre_piece = jnp.dot(
        x_piece, w_in, precision=lax.Precision.HIGHEST, preferred_element_type=jnp.float32
    )
    act_piece = contract_last(out_piece, w_out)
    pre_sum, grad_act = lax.psum((pre_piece, act_piece), "narrow")
    act, slope = gelu_parts(pre_sum + b_in)
    grad_pre = grad_act * slope
    raw_in = contract_first(x_piece, grad_pre)
    raw_out = contract_first(act, out_piece)
    bias_in = jnp.sum(grad_pre, axis=0)
    bias_out = jnp.sum(out_piece, axis=0)
    squares = jnp.sum(raw_in * raw_in) + jnp.sum(raw_out * raw_out)
    token_count = x_tokens.shape[0] * lax.axis_size("wide")
    grad_in = lax.psum_scatter(
        contract_last(grad_pre, w_in), "wide", scatter_dimension=0, tiled=True
    )
    total = lax.psum(squares, ("wide", "narrow"))
    factor = jnp.minimum(1.0, jnp.sqrt(1.0 * D * FF * token_count) / (jnp.sqrt(total) + 1e-06))
    return (grad_in, raw_in * factor, raw_out * factor, bias_in * factor, bias_out * factor)


def solution(mesh):
    placed = (
        P("wide", "narrow"),
        P("wide", "narrow"),
        P("narrow", "wide"),
        P("wide"),
        P("wide", "narrow"),
    )
    return jax.shard_map(
        local,
        mesh=mesh,
        in_specs=placed,
        out_specs=(
            P("wide", "narrow"),
            P("narrow", "wide"),
            P("wide", "narrow"),
            P("wide"),
            P("narrow"),
        ),
        check_vma=False,
    )
```

profile of v0, /device:TPU:1, one launch (start us, length us, event | category | flops | bytes accessed | tf_op | source)
XLA Modules:
  0.0 433.7 jit_solution(1132948923682249653)
XLA Ops:
  7.2 0.0 copy-start
  7.2 0.0 all-gather.3.cloned.1.call-start
  7.2 0.7 all-gather.3.cloned.1.call-update
  7.9 0.0 all-gather.5.cloned.1.call-start
  8.0 0.7 all-gather.5.cloned.1.call-update
  8.7 0.0 all-reduce.3.cloned.1.call-start
  8.7 92.3 %all-gather.3.cloned.1.call-done = f32[512,768]{1,0:T(8,128)} async-done(((f32[8,768]{1,0:T(8,128)}), f32[512,768]{1,0:T(8,128)}) %all-gather.3.cloned.1.call-update) | async-done | bytes 1572880 | tf_op jit(solution)/shard_map/all_gather | solution.py:47
  101.0 5.3 %fusion.23 = f32[512,384]{1,0:T(8,128)} fusion(f32[512,768]{1,0:T(8,128)} %all-gather.3.cloned.1.call-done, f32[384,768]{1,0:T(8,128)} %param.9), kind=kOutput, calls=%fused_computation.29 | convolution fusion | flops 1811939328 | bytes 3538944 | tf_op jit(solution)/shard_map/dot_general | solution.py:37
  106.3 78.0 %all-gather.5.cloned.1.call-done = f32[512,768]{1,0:T(8,128)} async-done(((f32[8,768]{1,0:T(8,128)}), f32[512,768]{1,0:T(8,128)}) %all-gather.5.cloned.1.call-update) | async-done | bytes 1572880 | tf_op jit(solution)/shard_map/all_gather | solution.py:47
  184.3 0.0 copy-done
  184.3 4.9 %fusion.24 = f32[512,384]{1,0:T(8,128)} fusion(f32[512,768]{1,0:T(8,128)} %all-gather.5.cloned.1.call-done, f32[768,384]{1,0:T(8,128)S(1)} %copy-done), kind=kOutput, calls=%fused_computation.30 | convolution fusion | flops 1811939328 | bytes 3538944 | tf_op jit(solution)/shard_map/dot_general | solution.py:48
  189.2 0.0 copy-start.3
  189.2 0.0 all-reduce.3.cloned.1.call-update
  189.2 0.2 reduce-scatter.2.cloned.1.call-start
  189.4 81.7 %all-reduce.3.cloned.1.call-done = (f32[512,384]{1,0:T(8,128)}, f32[512,384]{1,0:T(8,128)}) async-done(((f32[512,384]{1,0:T(8,128)}, f32[512,384]{1,0:T(8,128)}), (f32[512,384]{1,0:T(8,128)}, f32[512,384]{1,0:T(8,128)})) %all-reduce.3.cloned.1.call-update) | async-done | bytes 1572880 | tf_op jit(solution)/shard_map/psum | solution.py:52
  271.1 0.0 copy-done.3
  271.1 1.9 fusion.21
  273.0 3.8 fusion.25
  276.9 0.0 reduce-scatter.2.cloned.1.call-update
  276.9 0.0 copy-start.1
  276.9 0.0 copy-start.2
  276.9 5.3 %multiply_reduce_fusion.1 = (f32[]{:T(128)}, f32[384,768]{1,0:T(8,128)}) fusion(f32[512,384]{1,0:T(8,128)S(1)} %get-tuple-element.13, f32[512,768]{1,0:T(8,128)} %all-gather.5.cloned.1.call-done), kind=kOutput, calls=%fused_computation.4 | convolution fusion | flops 1812529152 | bytes 3538948 | tf_op jit(solution)/shard_map/dot_general | solution.py:27
  282.3 0.0 copy-done.1
  282.3 0.0 copy-done.2
  282.3 4.0 multiply_reduce_fusion
  287.6 0.1 reduce_sum.39
  287.7 102.1 %psum.23 = f32[]{:T(128)} all-reduce(f32[]{:T(128)S(6)} %add.41), channel_id=1, replica_groups=mesh['wide'=64,'narrow'=8] {'wide','narrow'}, use_global_device_ids=true, to_apply=%region_5.0 | all-reduce | flops 1 | bytes 8 | tf_op jit(solution)/shard_map/psum | solution.py:64
  390.5 2.8 multiply_bitcast_fusion
  393.3 1.4 copy.10
  394.7 0.6 broadcast_multiply_fusion.2
  395.3 0.6 broadcast_multiply_fusion.1
  395.9 31.3 %reduce-scatter.2.cloned.1.call-done = f32[8,768]{1,0:T(8,128)} async-done(((f32[512,768]{1,0:T(8,128)}), f32[8,768]{1,0:T(8,128)}) %reduce-scatter.2.cloned.1.call-update) | async-done | bytes 24592 | tf_op jit(solution)/shard_map/reduce_scatter | solution.py:61
Async XLA Ops:
  7.2 177.1 %copy-start = (f32[768,384]{1,0:T(8,128)S(1)}, f32[768,384]{1,0:T(8,128)}, u32[]{:S(2)}) copy-start(f32[768,384]{1,0:T(8,128)} %param.7) | copy-start | bytes 3538948
  7.2 93.8 %all-gather.3.cloned.1.call-start = ((), (), s32[]{:S(2)}) async-start(), calls=%async_computation.1 | async-start | bytes 1597440 | tf_op jit(solution)/shard_map/all_gather | solution.py:47
  7.9 176.3 %all-gather.5.cloned.1.call-start = ((), (), s32[]{:S(2)}) async-start(), calls=%async_computation.2 | async-start | bytes 1597440 | tf_op jit(solution)/shard_map/all_gather | solution.py:47
  8.7 262.5 %all-reduce.3.cloned.1.call-start = ((), (), s32[]{:S(2)}) async-start(), calls=%async_computation.4 | async-start | bytes 3145728 | tf_op jit(solution)/shard_map/psum | solution.py:52
  189.2 82.0 %copy-start.3 = (f32[384]{0:T(512)S(1)}, f32[384]{0:T(512)}, u32[]{:S(2)}) copy-start(f32[384]{0:T(512)} %param.8) | copy-start | bytes 4612
  189.2 237.9 %reduce-scatter.2.cloned.1.call-start = ((), (), s32[]{:S(2)}) async-start(), calls=%async_computation.3 | async-start | bytes 1597440 | tf_op jit(solution)/shard_map/reduce_scatter | solution.py:61
  276.9 5.3 %copy-start.1 = (f32[512,768]{1,0:T(8,128)S(1)}, f32[512,768]{1,0:T(8,128)}, u32[]{:S(2)}) copy-start(f32[512,768]{1,0:T(8,128)} %all-gather.3.cloned.1.call-done) | copy-start | bytes 4718596
  276.9 5.3 %copy-start.2 = (f32[512,384]{1,0:T(8,128)S(1)}, f32[512,384]{1,0:T(8,128)}, u32[]{:S(2)}) copy-start(f32[512,384]{1,0:T(8,128)} %get-tuple-element.11) | copy-start | bytes 2359300
Sparse Core Ops, SparseCore 0:
  11.4 89.6 all-gather.2
  104.4 79.8 all-gather.4
  189.3 81.7 all-reduce.2
  277.0 150.0 reduce-scatter.1
where the time goes:
time: 438 us; the launch traced here: 434 us
  waiting for transfers between devices  285 us (65%)
  blocking collectives  102 us (23%)
  matrix products  23.3 us (5%)
  between operations  15.8 us (4%)
  other arithmetic  6.03 us (1%)
    all_gather x2, waiting for transfers between devices, local(): lax.all_gather((x_tokens, grad_out), 'wide', axis=0, tiled=True)  170 us
    psum x1, blocking collectives, local(): total = lax.psum(squares, ('wide', 'narrow'))  102 us
    psum x1, waiting for transfers between devices, local(): pre_sum, grad_act = lax.psum((pre_piece, act_piece), 'narrow')  81.7 us
    reduce_scatter x1, waiting for transfers between devices, local(): lax.psum_scatter(contract_last(grad_pre, w_in), 'wide', scatter_dimension...  31.3 us
    dot_general x2, matrix products, contract_first(): lax.dot_general(left, right, (((0,), (0,)), ((), ())), precision=lax.Prec...  9.31 us
    dot_general x2, matrix products, contract_last(): lax.dot_general(left, right, (((1,), (1,)), ((), ())), precision=lax.Prec...  9.11 us
  transfers between devices with their start and end apart: 4, of which 4 were waited for; matrix products, arithmetic and copies ran while one was open for 5% of the time, Pallas kernels for 0%

commit v1 on v0

v1 whole, which is shorter than its diff:
```python
import math

import jax
import jax.numpy as jnp
from jax import lax
from jax.experimental import pallas as pl
from jax.experimental.pallas import tpu as pltpu
from jax.sharding import PartitionSpec as P

D = 6144
FF = 24576
TOKENS = 512
MESH = pl.DeviceIdType.MESH
F32, BF16 = jnp.float32, jnp.bfloat16

NZ, NY, NC, NN = 8, 4, 2, 8
ROWS = 8
BLOCK = NY * NC * ROWS
SENDS = (2, 6, 1, 3, 5, 7, 4)
GROUPS = ((0, 1), (1, 2), (3, 2), (5, 2), (7, 1))
PLACES = ((1, 128), (0, 0), (0, 128), (1, 0), (1, 192))
HALF = 256
FEAT, HID = 768, 384

tanh_scale = math.sqrt(2.0 / math.pi)
cubic_weight = 0.044715


def gelu_parts(pre):
    inner = tanh_scale * (pre + cubic_weight * pre * pre * pre)
    tangent = jnp.tanh(inner)
    value = 0.5 * pre * (1.0 + tangent)
    slope = 0.5 * (1.0 + tangent) + 0.5 * pre * (1.0 - tangent * tangent) * tanh_scale * (
        1.0 + 3.0 * cubic_weight * pre * pre
    )
    return (value, slope)


def split(values):
    high = values.astype(BF16)
    return high, (values - high.astype(F32)).astype(BF16)


def product(left, right):
    return jnp.dot(left, right, preferred_element_type=F32)


def dot3(pair, high, low):
    rows = pair[0].shape[0]
    both = product(jnp.concatenate(pair, axis=0), high)
    return (both[:rows] + both[rows:]) + product(pair[0], low)


def remote(source, target, send, recv, wide, narrow):
    return pltpu.make_async_remote_copy(
        src_ref=source,
        dst_ref=target,
        send_sem=send,
        recv_sem=recv,
        device_id=(wide, narrow),
        device_id_type=MESH,
    )


def drain(ref, sem):
    pltpu.make_async_copy(ref, ref, sem).wait()


def kernel(
    x_ref, g_ref, w_in_ref, b_ref, w_out_ref,
    grad_in_ref, raw_in_ref, raw_out_ref, bias_in_ref, bias_out_ref, factor_ref,
    xg, part, from_narrow, ag, gi, gi_core, gi_z, gi_y, sums,
    w_in_f, w_out_f, w_in_h, w_in_l, w_out_h, w_out_l, w_back_h, w_back_l,
    x_across, g_along, p_along, a_across, bias, b_here,
    load_sem, y_send, y_recv, z_send, z_recv, c_send, c_recv,
    n_send, n_recv, a_send, a_recv, gc_send, gc_recv, gz_send, gz_recv, gy_send, gy_recv,
    s_send, s_recv,
):
    wide = lax.axis_index("wide")
    n = lax.axis_index("narrow")
    z = lax.div(wide, NY * NC)
    y = lax.rem(lax.div(wide, NC), NY)
    c = lax.rem(wide, NC)

    def at(zz, yy, cc):
        return (zz * NY + yy) * NC + cc

    load_in = pltpu.make_async_copy(w_in_ref, w_in_f, load_sem.at[0])
    load_out = pltpu.make_async_copy(w_out_ref, w_out_f, load_sem.at[1])
    load_x = pltpu.make_async_copy(x_ref, xg.at[0, z, c, y], load_sem.at[2])
    load_g = pltpu.make_async_copy(g_ref, xg.at[1, z, c, y], load_sem.at[3])
    load_b = pltpu.make_async_copy(b_ref, b_here, load_sem.at[4])
    for load in (load_x, load_g, load_in, load_out, load_b):
        load.start()

    plane = lax.rem(wide, NY * NC)
    barrier = pltpu.get_barrier_semaphore()
    for j in range(1, 8):
        for peer in (
            (wide, lax.rem(n + j, NN)),
            (z * NY * NC + lax.rem(plane + j, NY * NC), n),
            (lax.rem(z + j, NZ) * NY * NC + plane, n),
        ):
            pl.semaphore_signal(barrier, inc=1, device_id=peer, device_id_type=MESH)
    load_x.wait()
    load_g.wait()
    pl.semaphore_wait(barrier, 21)

    for j in (2, 1, 3):
        own = xg.at[:, z, c, y]
        remote(own, own, y_send, y_recv, at(z, lax.rem(y + j, NY), c), n).start()

    load_in.wait()
    w_in_h[...], w_in_l[...] = split(w_in_f[...])
    load_out.wait()
    w_out_h[...], w_out_l[...] = split(w_out_f[...].T)
    load_b.wait()

    drain(xg.at[:, z, c, pl.ds(0, 3)], y_recv)
    own = xg.at[:, z, c]
    remote(own, own, c_send, c_recv.at[0], at(z, y, 1 - c), n).start()
    remote(own, own, z_send, z_recv.at[1], at(lax.rem(z + 1, NZ), y, c), n).start()
    remote(own, own, z_send, z_recv.at[2], at(lax.rem(z + NZ - 1, NZ), y, c), n).start()

    def block_of(k):
        return lax.rem(z + NZ + (1 - 2 * (k % 2)) * ((k + 1) // 2), NZ)

    def arrive(group):
        first, count = GROUPS[group]
        for k in range(max(first, 1), first + count):
            zb = block_of(k)
            here = xg.at[:, zb, c]
            if k < 7:
                drain(here, z_recv.at[k])
                onward = at(lax.rem(z + NZ - 1 + 2 * (k % 2), NZ), y, c)
                passed = here if k < 5 else xg.at[k - 5, zb, c]
                remote(passed, passed, z_send, z_recv.at[k + 2], onward, n).start()
            else:
                drain(xg.at[0, zb, c], z_recv.at[7])
                drain(xg.at[1, zb, c], z_recv.at[8])
            remote(here, here, c_send, c_recv.at[k], at(z, y, 1 - c), n).start()

    def forward(group):
        first, count = GROUPS[group]
        turn, start = PLACES[group]
        size = count * BLOCK
        blocks = [block_of(k) for k in range(first, first + count)]
        for zb, k in zip(blocks, range(first, first + count)):
            drain(xg.at[:, zb, 1 - c], c_recv.at[k])
        g = jnp.concatenate([xg[1, zb].reshape(BLOCK, FEAT) for zb in blocks], axis=0)
        g_pair = split(g)
        grad_act = dot3(g_pair, w_out_h[...], w_out_l[...])
        x = jnp.concatenate([xg[0, zb].reshape(BLOCK, FEAT) for zb in blocks], axis=0)
        x_pair = split(x)
        pre = dot3(x_pair, w_in_h[...], w_in_l[...])
        for b in range(count):
            rows = slice(b * BLOCK, (b + 1) * BLOCK)
            part[:, first + b, 0] = pre[rows].reshape(NN, ROWS, HID)
            part[:, first + b, 1] = grad_act[rows].reshape(NN, ROWS, HID)
        some = pl.ds(first, count)
        for j in SENDS:
            peer = lax.rem(n + j, NN)
            remote(
                part.at[peer, some], from_narrow.at[j - 1, some], n_send, n_recv.at[group], wide, peer
            ).start()
        across = split(x.T)
        for third, which in enumerate((0, 1, 0)):
            x_across[turn, :, HALF * third + start:HALF * third + start + size] = across[which]
        for third, which in enumerate((0, 0, 1)):
            g_along[turn, HALF * third + start:HALF * third + start + size, :] = g_pair[which]

    def activate(group):
        first, count = GROUPS[group]
        some = pl.ds(first, count)
        drain(from_narrow.at[:, some], n_recv.at[group])
        total = part[n, some]
        for j in range(7):
            total = total + from_narrow[j, some]
        act, slope = gelu_parts(total[:, 0] + b_here[...])
        ag[n, some, 0] = act
        ag[n, some, 1] = total[:, 1] * slope
        mine = ag.at[n, some]
        for j in SENDS:
            remote(mine, mine, a_send, a_recv.at[group], wide, lax.rem(n + j, NN)).start()

    def backward(group):
        first, count = GROUPS[group]
        turn, start = PLACES[group]
        size = count * BLOCK
        drain(ag.at[pl.ds(0, 7), pl.ds(first, count)], a_recv.at[group])
        grad_pre = jnp.concatenate(
            [ag[:, k, 1].reshape(BLOCK, HID) for k in range(first, first + count)], axis=0
        )
        pair = split(grad_pre)
        grad = dot3(pair, w_back_h[...], w_back_l[...])
        gi[pl.ds(first, count)] = grad.reshape(count, NC, NY, ROWS, FEAT)
        some = pl.ds(first, count)
        remote(
            gi.at[some, 1 - c], gi_core.at[some], gc_send, gc_recv.at[group], at(z, y, 1 - c), n
        ).start()
        bias[...] += jnp.sum(grad_pre.reshape(size // 8, 8, HID), axis=0)
        act = jnp.concatenate(
            [ag[:, k, 0].reshape(BLOCK, HID) for k in range(first, first + count)], axis=0
        )
        across = split(act.T)
        for third, which in enumerate((0, 1, 0)):
            a_across[turn, :, HALF * third + start:HALF * third + start + size] = across[which]
        for third, which in enumerate((0, 0, 1)):
            p_along[turn, HALF * third + start:HALF * third + start + size, :] = pair[which]

    def hand_over(group):
        first, count = GROUPS[group]
        drain(gi_core.at[pl.ds(first, count)], gc_recv.at[group])
        for k in range(first, first + count):
            gi[k, c] += gi_core[k]
            if k > 0:
                remote(
                    gi.at[k, c], gi_z.at[k - 1], gz_send, gz_recv, at(block_of(k), y, c), n
                ).start()

    def to_vreg(squares):
        rows, columns = squares.shape
        lanes = jnp.sum(squares.reshape(rows // 8, 8, columns), axis=0)
        out = lanes[:, :128]
        for j in range(1, columns // 128):
            out = out + lanes[:, 128 * j:128 * (j + 1)]
        return out

    def weight_round(turn, size, across, along, raw):
        total = jnp.zeros((8, 128), F32)
        for start in range(0, raw.shape[0], size):
            rows = slice(start, start + size)
            tile = product(across[turn, rows, :], along[turn])
            if turn == 1:
                tile = tile + raw[rows, :]
                total = total + to_vreg(tile * tile)
            raw[rows, :] = tile
        return total

    bias[...] = jnp.zeros_like(bias)
    forward(0)
    arrive(1)
    w_back_h[...], w_back_l[...] = split(w_in_f[...].T)
    forward(1)
    activate(0)
    arrive(2)
    forward(2)
    backward(0)
    activate(1)
    arrive(3)
    forward(3)
    hand_over(0)
    backward(1)
    arrive(4)
    activate(2)
    forward(4)
    hand_over(1)
    backward(2)
    activate(3)
    hand_over(2)
    weight_round(0, 256, x_across, p_along, raw_in_ref)
    weight_round(0, 128, a_across, g_along, raw_out_ref)
    activate(4)
    backward(3)
    hand_over(3)
    backward(4)
    total = weight_round(1, 256, x_across, p_along, raw_in_ref)
    hand_over(4)
    total = total + weight_round(1, 128, a_across, g_along, raw_out_ref)

    def share(phase, place, value, peers):
        sums[phase, place] = value
        for peer in peers:
            slot = sums.at[phase, place]
            remote(slot, slot, s_send, s_recv.at[phase], *peer).start()

    def collect(phase):
        drain(sums.at[phase, pl.ds(0, 7)], s_recv.at[phase])
        return jnp.sum(sums[phase], axis=0)

    share(0, n, total, [(wide, lax.rem(n + j, NN)) for j in range(1, 8)])

    drain(gi_z, gz_recv)
    own_sum = gi[0, c]
    for j in range(7):
        own_sum = own_sum + gi_z[j]
    gi[0, c] = own_sum
    for j in (2, 1, 3):
        to = lax.rem(y + j, NY)
        remote(gi.at[0, c, to], gi_y.at[j - 1], gy_send, gy_recv, at(z, to, c), n).start()

    total = collect(0)
    share(1, plane, total, [
        (z * NY * NC + lax.rem(plane + j, NY * NC), n) for j in range(1, 8)
    ])
    bias_in_ref[...] = jnp.sum(bias[...], axis=0, keepdims=True)
    bias_out_ref[...] = jnp.sum(xg[1].reshape(TOKENS, FEAT), axis=0, keepdims=True)
    total = collect(1)
    share(2, z, total, [
        (lax.rem(z + j, NZ) * NY * NC + plane, n) for j in range(1, 8)
    ])
    drain(gi_y, gy_recv)
    grad_in_ref[...] = (gi[0, c, y] + gi_y[0]) + (gi_y[1] + gi_y[2])
    drain(xg.at[:, z, c, pl.ds(0, 3)], y_send)
    drain(xg.at[:, pl.ds(0, 7), 0], z_send)
    drain(xg.at[:, :, 0], c_send)
    drain(from_narrow, n_send)
    drain(ag.at[pl.ds(0, 7)], a_send)
    drain(gi_core, gc_send)
    drain(gi_z, gz_send)
    drain(gi_y, gy_send)
    total = jnp.sum(collect(2), keepdims=True)
    factor = jnp.minimum(1.0, math.sqrt(1.0 * D * FF * TOKENS) / (jnp.sqrt(total) + 1e-06))
    factor_ref[...] = jnp.broadcast_to(factor, factor_ref.shape)
    drain(sums.at[:, pl.ds(0, 7)], s_send)


PIECES = 3


def scale_kernel(
    grad_in_ref, raw_in_ref, raw_out_ref, bias_in_ref, bias_out_ref, factor_ref,
    grad_in_out, gw_in, gw_out, gb_in, gb_out, buf_in, buf_out, sems,
):
    factor = factor_ref[0:1, 0:1]
    stores = []
    for which, (raw, buf, out) in enumerate(
        ((raw_in_ref, buf_in, gw_in), (raw_out_ref, buf_out, gw_out))
    ):
        size = raw.shape[0] // PIECES
        for i in range(PIECES):
            rows = pl.ds(i * size, size)
            buf[rows, :] = raw[rows, :] * factor
            store = pltpu.make_async_copy(buf.at[rows], out.at[rows], sems.at[which, i])
            store.start()
            stores.append(store)
    grad_in_out[...] = grad_in_ref[...]
    gb_in[...] = (bias_in_ref[...] * factor)[0]
    gb_out[...] = (bias_out_ref[...] * factor)[0]
    for store in stores:
        store.wait()


def local(x_tokens, grad_out, w_in, b_in, w_out):
    vmem = pl.BlockSpec(memory_space=pltpu.VMEM)
    anywhere = pl.BlockSpec(memory_space=pl.ANY)
    dma = pltpu.SemaphoreType.DMA
    grad_in, raw_in, raw_out, bias_in, bias_out, factor = pl.pallas_call(
        kernel,
        out_shape=(
            jax.ShapeDtypeStruct((ROWS, FEAT), F32),
            jax.ShapeDtypeStruct((FEAT, HID), F32),
            jax.ShapeDtypeStruct((HID, FEAT), F32),
            jax.ShapeDtypeStruct((1, HID), F32),
            jax.ShapeDtypeStruct((1, FEAT), F32),
            jax.ShapeDtypeStruct((8, 128), F32),
        ),
        in_specs=[pl.BlockSpec(memory_space=pltpu.HBM)] * 5,
        out_specs=(vmem, vmem, vmem, vmem, vmem, vmem),
        scratch_shapes=[
            pltpu.VMEM((2, NZ, NC, NY, ROWS, FEAT), F32),
            pltpu.VMEM((NN, NZ, 2, ROWS, HID), F32),
            pltpu.VMEM((NN - 1, NZ, 2, ROWS, HID), F32),
            pltpu.VMEM((NN, NZ, 2, ROWS, HID), F32),
            pltpu.VMEM((NZ, NC, NY, ROWS, FEAT), F32),
            pltpu.VMEM((NZ, NY, ROWS, FEAT), F32),
            pltpu.VMEM((NZ - 1, NY, ROWS, FEAT), F32),
            pltpu.VMEM((NY - 1, ROWS, FEAT), F32),
            pltpu.VMEM((3, 8, 8, 128), F32),
            pltpu.VMEM((FEAT, HID), F32),
            pltpu.VMEM((HID, FEAT), F32),
            pltpu.VMEM((FEAT, HID), BF16),
            pltpu.VMEM((FEAT, HID), BF16),
            pltpu.VMEM((FEAT, HID), BF16),
            pltpu.VMEM((FEAT, HID), BF16),
            pltpu.VMEM((HID, FEAT), BF16),
            pltpu.VMEM((HID, FEAT), BF16),
            pltpu.VMEM((2, FEAT, 3 * HALF), BF16),
            pltpu.VMEM((2, 3 * HALF, FEAT), BF16),
            pltpu.VMEM((2, 3 * HALF, HID), BF16),
            pltpu.VMEM((2, HID, 3 * HALF), BF16),
            pltpu.VMEM((ROWS, HID), F32),
            pltpu.VMEM((HID,), F32),
            dma((5,)),
            dma, dma,
            dma, dma((9,)),
            dma, dma((NZ,)),
            dma, dma((NZ,)),
            dma, dma((NZ,)),
            dma, dma((NZ,)),
            dma, dma,
            dma, dma,
            dma, dma((3,)),
        ],
        compiler_params=pltpu.CompilerParams(
            collective_id=0, has_side_effects=True, vmem_limit_bytes=51 * 1024 * 1024
        ),
    )(x_tokens, grad_out, w_in, b_in, w_out)
    return pl.pallas_call(
        scale_kernel,
        out_shape=(
            jax.ShapeDtypeStruct((ROWS, FEAT), F32),
            jax.ShapeDtypeStruct((FEAT, HID), F32),
            jax.ShapeDtypeStruct((HID, FEAT), F32),
            jax.ShapeDtypeStruct((HID,), F32),
            jax.ShapeDtypeStruct((FEAT,), F32),
        ),
        in_specs=[vmem, vmem, vmem, vmem, vmem, vmem],
        out_specs=(vmem, anywhere, anywhere, vmem, vmem),
        scratch_shapes=[
            pltpu.VMEM((FEAT, HID), F32),
            pltpu.VMEM((HID, FEAT), F32),
            dma((2, PIECES)),
        ],
        compiler_params=pltpu.CompilerParams(vmem_limit_bytes=16 * 1024 * 1024),
    )(grad_in, raw_in, raw_out, bias_in, bias_out, factor)


def solution(mesh):
    placed = (
        P("wide", "narrow"),
        P("wide", "narrow"),
        P("narrow", "wide"),
        P("wide"),
        P("wide", "narrow"),
    )
    return jax.shard_map(
        local,
        mesh=mesh,
        in_specs=placed,
        out_specs=(
            P("wide", "narrow"),
            P("narrow", "wide"),
            P("wide", "narrow"),
            P("wide"),
            P("narrow"),
        ),
        check_vma=False,
    )
```

time: 438 us -> 96.3 us (0.22)
  waiting for transfers between devices: 285 us -> 0 us
  blocking collectives: 102 us -> 0 us
  Pallas kernels: 0 us -> 93.2 us
  matrix products: 23.3 us -> 0 us
  between operations: 15.8 us -> 0.65 us
  other arithmetic: 6.03 us -> 0 us
    all_gather x2 -> x0, waiting for transfers between devices: 170 us -> none  [local(): lax.all_gather((x_tokens, grad_out), 'wide', axis=0, tiled=True)]
    psum x1 -> x0, blocking collectives: 102 us -> none  [local(): total = lax.psum(squares, ('wide', 'narrow'))]
    pallas_call x0 -> x2, Pallas kernels: none -> 93.2 us  [the longest x1 91.1 us: local(): pl.pallas_call(kernel, out_shape=(jax.ShapeDtypeStruct((ROWS, FEAT), F32)...]
    psum x1 -> x0, waiting for transfers between devices: 81.7 us -> none  [local(): pre_sum, grad_act = lax.psum((pre_piece, act_piece), 'narrow')]
    reduce_scatter x1 -> x0, waiting for transfers between devices: 31.3 us -> none  [local(): lax.psum_scatter(contract_last(grad_pre, w_in), 'wide', scatter_dimension...]
    dot_general x5 -> x0, matrix products: 23.3 us -> none  [the longest x2 9.31 us: contract_first(): lax.dot_general(left, right, (((0,), (0,)), ((), ())), precision=lax.Prec...]
  transfers between devices with their start and end apart: 4 -> 0, of which waited for: 4 -> 0; matrix products, arithmetic and copies ran while one was open for 5% -> 0% of each run, Pallas kernels for 0% -> 0%
where the time goes in v1:
time: 96.3 us; the launch traced here: 96 us
  Pallas kernels  93.2 us (97%)
  local copies, waits for them, and re-layouts  2.15 us (2%)
    pallas_call x1, Pallas kernels, local(): pl.pallas_call(kernel, out_shape=(jax.ShapeDtypeStruct((ROWS, FEAT), F32)...  91.1 us
    unnamed x6, local copies, waits for them, and re-layouts  2.15 us
    pallas_call x1, Pallas kernels, local(): pl.pallas_call(scale_kernel, out_shape=(jax.ShapeDtypeStruct((ROWS, FEAT)...  2.12 us

profile of v1, /device:TPU:1, one launch (start us, length us, event | category | flops | bytes accessed | tf_op | source)
XLA Modules:
  0.0 96.0 jit_solution(10401468419623447544)
XLA Ops:
  0.6 0.0 copy-start
  0.6 0.7 copy-done
  1.4 0.0 copy-start.1
  1.4 0.7 copy-done.1
  2.1 0.0 copy-start.2
  2.1 0.7 copy-done.2
  2.8 91.1 %shard_map.92 = (f32[8,768]{1,0:T(8,128)S(1)}, f32[768,384]{1,0:T(8,128)S(1)}, f32[384,768]{1,0:T(8,128)S(1)}, f32[1,384]{1,0:T(1,128)S(1)}, f32[1,768]{1,0:T(1,128)S(1)}, /*index=5*/f32[8,128]{1,0:T(8,128)S(1)}) custom-call(f32[8,768]{1,0:T(8,128)S(1)} %copy-done, f32[8,768]{1,0:T(8,128)S(1)} %copy-done.1, f32[768,384]{1,0:T(8,128)} %w_in_ref.1, ...), custom_call_target="tpu_custom_call" | custom-call | tf_op jit(solution)/shard_map/pallas_call | solution.py:348
  93.9 2.1 %shard_map.93 = (f32[8,768]{1,0:T(8,128)}, f32[768,384]{1,0:T(8,128)}, f32[384,768]{1,0:T(8,128)}, f32[384]{0:T(512)}, f32[768]{0:T(1024)}) custom-call(f32[8,768]{1,0:T(8,128)S(1)} %get-tuple-element.11.grad_in_ref, f32[768,384]{1,0:T(8,128)S(1)} %get-tuple-element.12.raw_in_ref, f32[384,768]{1,0:T(8,128)S(1)} %get-tuple-element.13.raw_out_ref, ...), custom_call_target="tpu_custom_call" | custom-call | tf_op jit(solution)/shard_map/pallas_call | solution.py:399
Async XLA Ops:
  0.6 0.7 copy-start
  1.4 0.7 copy-start.1
  2.1 0.7 copy-start.2

commit v2 on v1

--- a/solution.py
+++ b/solution.py
@@ -16,10 +16,14 @@
 NZ, NY, NC, NN = 8, 4, 2, 8
 ROWS = 8
 BLOCK = NY * NC * ROWS
-SENDS = (2, 6, 1, 3, 5, 7, 4)
+NX = 4
 GROUPS = ((0, 1), (1, 2), (3, 2), (5, 2), (7, 1))
 PLACES = ((1, 128), (0, 0), (0, 128), (1, 0), (1, 192))
 HALF = 256
+FIRST_Y = 5
+STEPS = (
+    "10a1200130a2", "11024021a312", "3103a4504122", "041332605114", "702342613352", "247143346253",
+)
 FEAT, HID = 768, 384
 
 tanh_scale = math.sqrt(2.0 / math.pi)
@@ -69,11 +73,12 @@
 def kernel(
     x_ref, g_ref, w_in_ref, b_ref, w_out_ref,
     grad_in_ref, raw_in_ref, raw_out_ref, bias_in_ref, bias_out_ref, factor_ref,
-    xg, part, from_narrow, ag, gi, gi_core, gi_z, gi_y, sums,
+    xg, part, relay, near, across_y, ag, gi, gi_core, gi_z, gi_y, gi_y_first, gi_z_last, sums,
     w_in_f, w_out_f, w_in_h, w_in_l, w_out_h, w_out_l, w_back_h, w_back_l,
     x_across, g_along, p_along, a_across, bias, b_here,
     load_sem, y_send, y_recv, z_send, z_recv, c_send, c_recv,
-    n_send, n_recv, a_send, a_recv, gc_send, gc_recv, gz_send, gz_recv, gy_send, gy_recv,
+    f_send, f_recv, n_send, n_recv, s_y_send, s_y_recv, a_send, a_y_recv, a_one_recv, a_two_recv, a_far_recv,
+    gc_send, gc_recv, gz_send, gz_recv, gy_send, gy_recv, gyf_send, gyf_recv, gzl_send, gzl_recv,
     s_send, s_recv,
 ):
     wide = lax.axis_index("wide")
@@ -81,6 +86,11 @@
     z = lax.div(wide, NY * NC)
     y = lax.rem(lax.div(wide, NC), NY)
     c = lax.rem(wide, NC)
+
+    yl = lax.div(n, NX)
+    x = lax.rem(n, NX)
+    right, left, far = (lax.rem(x + j, NX) for j in (1, 3, 2))
+    over = (1 - yl) * NX + x
 
     def at(zz, yy, cc):
         return (zz * NY + yy) * NC + cc
@@ -147,47 +157,85 @@
         blocks = [block_of(k) for k in range(first, first + count)]
         for zb, k in zip(blocks, range(first, first + count)):
             drain(xg.at[:, zb, 1 - c], c_recv.at[k])
-        g = jnp.concatenate([xg[1, zb].reshape(BLOCK, FEAT) for zb in blocks], axis=0)
-        g_pair = split(g)
+        g_rows = jnp.concatenate([xg[1, zb].reshape(BLOCK, FEAT) for zb in blocks], axis=0)
+        g_pair = split(g_rows)
         grad_act = dot3(g_pair, w_out_h[...], w_out_l[...])
-        x = jnp.concatenate([xg[0, zb].reshape(BLOCK, FEAT) for zb in blocks], axis=0)
-        x_pair = split(x)
+        x_rows = jnp.concatenate([xg[0, zb].reshape(BLOCK, FEAT) for zb in blocks], axis=0)
+        x_pair = split(x_rows)
         pre = dot3(x_pair, w_in_h[...], w_in_l[...])
         for b in range(count):
             rows = slice(b * BLOCK, (b + 1) * BLOCK)
             part[:, first + b, 0] = pre[rows].reshape(NN, ROWS, HID)
             part[:, first + b, 1] = grad_act[rows].reshape(NN, ROWS, HID)
         some = pl.ds(first, count)
-        for j in SENDS:
-            peer = lax.rem(n + j, NN)
-            remote(
-                part.at[peer, some], from_narrow.at[j - 1, some], n_send, n_recv.at[group], wide, peer
-            ).start()
-        across = split(x.T)
+        to_right, to_left = yl * NX + right, yl * NX + left
+        remote(part.at[far, some], relay.at[0, some], f_send, f_recv.at[group], wide, to_right).start()
+        remote(part.at[NX + far, some], relay.at[1, some], f_send, f_recv.at[group], wide, to_left).start()
+        remote(part.at[NX + right, some], near.at[0, 1, some], n_send, n_recv.at[group], wide, to_right).start()
+        remote(part.at[left, some], near.at[1, 0, some], n_send, n_recv.at[group], wide, to_left).start()
+        across = split(x_rows.T)
         for third, which in enumerate((0, 1, 0)):
             x_across[turn, :, HALF * third + start:HALF * third + start + size] = across[which]
         for third, which in enumerate((0, 0, 1)):
             g_along[turn, HALF * third + start:HALF * third + start + size, :] = g_pair[which]
 
+    def pass_on(group):
+        some = pl.ds(*GROUPS[group])
+        drain(relay.at[:, some], f_recv.at[group])
+        part[right, some] += relay[0, some]
+        part[NX + left, some] += relay[1, some]
+        remote(
+            part.at[right, some], near.at[0, 0, some], n_send, n_recv.at[group], wide, yl * NX + right
+        ).start()
+        remote(
+            part.at[NX + left, some], near.at[1, 1, some], n_send, n_recv.at[group], wide, yl * NX + left
+        ).start()
+
+    def add_x(group):
+        some = pl.ds(*GROUPS[group])
+        drain(near.at[:, :, some], n_recv.at[group])
+        part[over, some] += near[0, 1 - yl, some] + near[1, 1 - yl, some]
+        remote(
+            part.at[over, some], across_y.at[some], s_y_send, s_y_recv.at[group], wide, over
+        ).start()
+        part[n, some] += near[0, yl, some] + near[1, yl, some]
+
     def activate(group):
-        first, count = GROUPS[group]
-        some = pl.ds(first, count)
-        drain(from_narrow.at[:, some], n_recv.at[group])
-        total = part[n, some]
-        for j in range(7):
-            total = total + from_narrow[j, some]
+        some = pl.ds(*GROUPS[group])
+        drain(across_y.at[some], s_y_recv.at[group])
+        total = part[n, some] + across_y[some]
         act, slope = gelu_parts(total[:, 0] + b_here[...])
         ag[n, some, 0] = act
         ag[n, some, 1] = total[:, 1] * slope
         mine = ag.at[n, some]
-        for j in SENDS:
-            remote(mine, mine, a_send, a_recv.at[group], wide, lax.rem(n + j, NN)).start()
+        remote(mine, mine, a_send, a_y_recv.at[group], wide, over).start()
+        for side in (right, left):
+            remote(mine, mine, a_send, a_one_recv.at[group], wide, yl * NX + side).start()
+
+    ahead = lax.rem(x + 1 + 2 * yl, NX)
+    behind = lax.rem(x + 3 - 2 * yl, NX)
+
+    def spread(group):
+        some = pl.ds(*GROUPS[group])
+        drain(across_y.at[some], a_y_recv.at[group])
+        other = ag.at[over, some]
+        for side in (right, left):
+            remote(other, other, a_send, a_two_recv.at[group], wide, yl * NX + side).start()
+        drain(ag.at[pl.ds(0, 2), some], a_one_recv.at[group])
+        chunk = ag.at[yl * NX + behind, some]
+        remote(chunk, chunk, a_send, a_far_recv.at[group], wide, yl * NX + ahead).start()
+
+    def spread_far(group):
+        some = pl.ds(*GROUPS[group])
+        drain(ag.at[pl.ds(0, 2), some], a_two_recv.at[group])
+        chunk = ag.at[(1 - yl) * NX + ahead, some]
+        remote(chunk, chunk, a_send, a_far_recv.at[group], wide, yl * NX + behind).start()
 
     def backward(group):
         first, count = GROUPS[group]
         turn, start = PLACES[group]
         size = count * BLOCK
-        drain(ag.at[pl.ds(0, 7), pl.ds(first, count)], a_recv.at[group])
+        drain(ag.at[pl.ds(0, 2), pl.ds(first, count)], a_far_recv.at[group])
         grad_pre = jnp.concatenate(
             [ag[:, k, 1].reshape(BLOCK, HID) for k in range(first, first + count)], axis=0
         )
@@ -213,10 +261,28 @@
         drain(gi_core.at[pl.ds(first, count)], gc_recv.at[group])
         for k in range(first, first + count):
             gi[k, c] += gi_core[k]
-            if k > 0:
+            if 0 < k < FIRST_Y:
                 remote(
                     gi.at[k, c], gi_z.at[k - 1], gz_send, gz_recv, at(block_of(k), y, c), n
                 ).start()
+        if first >= FIRST_Y:
+            for j in (2, 1, 3):
+                to = lax.rem(y + j, NY)
+                remote(
+                    gi.at[pl.ds(first, count), c, to],
+                    gi_y_first.at[j - 1, pl.ds(first - FIRST_Y, count)],
+                    gyf_send, gyf_recv.at[group - 3], at(z, to, c), n,
+                ).start()
+
+    def to_owner(group):
+        first, count = GROUPS[group]
+        drain(gi_y_first.at[:, pl.ds(first - FIRST_Y, count)], gyf_recv.at[group - 3])
+        for k in range(first, first + count):
+            i = k - FIRST_Y
+            gi[k, c, y] += gi_y_first[0, i] + (gi_y_first[1, i] + gi_y_first[2, i])
+            remote(
+                gi.at[k, c, y], gi_z_last.at[i], gzl_send, gzl_recv, at(block_of(k), y, c), n
+            ).start()
 
     def to_vreg(squares):
         rows, columns = squares.shape
@@ -238,34 +304,25 @@
         return total
 
     bias[...] = jnp.zeros_like(bias)
-    forward(0)
-    arrive(1)
+    stages = {
+        "a": arrive, "0": forward, "1": pass_on, "2": add_x, "3": activate, "4": spread,
+        "5": spread_far, "6": backward, "7": hand_over, "8": to_owner,
+    }
+
+    def run(order):
+        for stage, group in zip(order[::2], order[1::2]):
+            stages[stage](int(group))
+
+    run("00")
     w_back_h[...], w_back_l[...] = split(w_in_f[...].T)
-    forward(1)
-    activate(0)
-    arrive(2)
-    forward(2)
-    backward(0)
-    activate(1)
-    arrive(3)
-    forward(3)
-    hand_over(0)
-    backward(1)
-    arrive(4)
-    activate(2)
-    forward(4)
-    hand_over(1)
-    backward(2)
-    activate(3)
-    hand_over(2)
+    for order in STEPS:
+        run(order)
     weight_round(0, 256, x_across, p_along, raw_in_ref)
+    run("4463725473")
     weight_round(0, 128, a_across, g_along, raw_out_ref)
-    activate(4)
-    backward(3)
-    hand_over(3)
-    backward(4)
+    run("6483")
     total = weight_round(1, 256, x_across, p_along, raw_in_ref)
-    hand_over(4)
+    run("74")
     total = total + weight_round(1, 128, a_across, g_along, raw_out_ref)
 
     def share(phase, place, value, peers):
@@ -280,9 +337,10 @@
 
     share(0, n, total, [(wide, lax.rem(n + j, NN)) for j in range(1, 8)])
 
+    to_owner(4)
     drain(gi_z, gz_recv)
     own_sum = gi[0, c]
-    for j in range(7):
+    for j in range(FIRST_Y - 1):
         own_sum = own_sum + gi_z[j]
     gi[0, c] = own_sum
     for j in (2, 1, 3):
@@ -300,15 +358,22 @@
         (lax.rem(z + j, NZ) * NY * NC + plane, n) for j in range(1, 8)
     ])
     drain(gi_y, gy_recv)
-    grad_in_ref[...] = (gi[0, c, y] + gi_y[0]) + (gi_y[1] + gi_y[2])
+    drain(gi_z_last, gzl_recv)
+    grad_in_ref[...] = ((gi[0, c, y] + gi_y[0]) + (gi_y[1] + gi_y[2])) + (
+        (gi_z_last[0] + gi_z_last[1]) + gi_z_last[2]
+    )
     drain(xg.at[:, z, c, pl.ds(0, 3)], y_send)
     drain(xg.at[:, pl.ds(0, 7), 0], z_send)
     drain(xg.at[:, :, 0], c_send)
-    drain(from_narrow, n_send)
+    drain(relay, f_send)
+    drain(near, n_send)
+    drain(across_y, s_y_send)
     drain(ag.at[pl.ds(0, 7)], a_send)
     drain(gi_core, gc_send)
     drain(gi_z, gz_send)
     drain(gi_y, gy_send)
+    drain(gi_y_first, gyf_send)
+    drain(gi_z_last, gzl_send)
     total = jnp.sum(collect(2), keepdims=True)
     factor = jnp.minimum(1.0, math.sqrt(1.0 * D * FF * TOKENS) / (jnp.sqrt(total) + 1e-06))
     factor_ref[...] = jnp.broadcast_to(factor, factor_ref.shape)
@@ -360,12 +425,16 @@
         scratch_shapes=[
             pltpu.VMEM((2, NZ, NC, NY, ROWS, FEAT), F32),
             pltpu.VMEM((NN, NZ, 2, ROWS, HID), F32),
-            pltpu.VMEM((NN - 1, NZ, 2, ROWS, HID), F32),
+            pltpu.VMEM((2, NZ, 2, ROWS, HID), F32),
+            pltpu.VMEM((2, 2, NZ, 2, ROWS, HID), F32),
+            pltpu.VMEM((NZ, 2, ROWS, HID), F32),
             pltpu.VMEM((NN, NZ, 2, ROWS, HID), F32),
             pltpu.VMEM((NZ, NC, NY, ROWS, FEAT), F32),
             pltpu.VMEM((NZ, NY, ROWS, FEAT), F32),
-            pltpu.VMEM((NZ - 1, NY, ROWS, FEAT), F32),
+            pltpu.VMEM((FIRST_Y - 1, NY, ROWS, FEAT), F32),
             pltpu.VMEM((NY - 1, ROWS, FEAT), F32),
+            pltpu.VMEM((NY - 1, NZ - FIRST_Y, ROWS, FEAT), F32),
+            pltpu.VMEM((NZ - FIRST_Y, ROWS, FEAT), F32),
             pltpu.VMEM((3, 8, 8, 128), F32),
             pltpu.VMEM((FEAT, HID), F32),
             pltpu.VMEM((HID, FEAT), F32),
@@ -385,10 +454,14 @@
             dma, dma,
             dma, dma((9,)),
             dma, dma((NZ,)),
-            dma, dma((NZ,)),
-            dma, dma((NZ,)),
-            dma, dma((NZ,)),
+            dma, dma((5,)),
+            dma, dma((5,)),
+            dma, dma((5,)),
+            dma, dma((5,)), dma((5,)), dma((5,)), dma((5,)),
+            dma, dma((5,)),
             dma, dma,
+            dma, dma,
+            dma, dma((2,)),
             dma, dma,
             dma, dma((3,)),
         ],

time: 96.3 us -> 95 us (0.987)
  Pallas kernels: 93.2 us -> 91.9 us
    pallas_call x1, Pallas kernels: 91.1 us -> 89.8 us  [local(): pl.pallas_call(kernel, out_shape=(jax.ShapeDtypeStruct((ROWS, FEAT), F32)...]
where the time goes in v2:
time: 95 us; the launch traced here: 94.7 us
  Pallas kernels  91.9 us (97%)
  local copies, waits for them, and re-layouts  2.15 us (2%)
    pallas_call x1, Pallas kernels, local(): pl.pallas_call(kernel, out_shape=(jax.ShapeDtypeStruct((ROWS, FEAT), F32)...  89.8 us
    unnamed x6, local copies, waits for them, and re-layouts  2.15 us
    pallas_call x1, Pallas kernels, local(): pl.pallas_call(scale_kernel, out_shape=(jax.ShapeDtypeStruct((ROWS, FEAT)...  2.12 us

profile of v2, /device:TPU:1, one launch (start us, length us, event | category | flops | bytes accessed | tf_op | source)
XLA Modules:
  0.0 94.7 jit_solution(16742572659850242996)
XLA Ops:
  0.6 0.0 copy-start
  0.6 0.7 copy-done
  1.4 0.0 copy-start.1
  1.4 0.7 copy-done.1
  2.1 0.0 copy-start.2
  2.1 0.7 copy-done.2
  2.8 89.8 %shard_map.92 = (f32[8,768]{1,0:T(8,128)S(1)}, f32[768,384]{1,0:T(8,128)S(1)}, f32[384,768]{1,0:T(8,128)S(1)}, f32[1,384]{1,0:T(1,128)S(1)}, f32[1,768]{1,0:T(1,128)S(1)}, /*index=5*/f32[8,128]{1,0:T(8,128)S(1)}) custom-call(f32[8,768]{1,0:T(8,128)S(1)} %copy-done, f32[8,768]{1,0:T(8,128)S(1)} %copy-done.1, f32[768,384]{1,0:T(8,128)} %w_in_ref.1, ...), custom_call_target="tpu_custom_call" | custom-call | tf_op jit(solution)/shard_map/pallas_call | solution.py:413
  92.6 2.1 %shard_map.93 = (f32[8,768]{1,0:T(8,128)}, f32[768,384]{1,0:T(8,128)}, f32[384,768]{1,0:T(8,128)}, f32[384]{0:T(512)}, f32[768]{0:T(1024)}) custom-call(f32[8,768]{1,0:T(8,128)S(1)} %get-tuple-element.11.grad_in_ref, f32[768,384]{1,0:T(8,128)S(1)} %get-tuple-element.12.raw_in_ref, f32[384,768]{1,0:T(8,128)S(1)} %get-tuple-element.13.raw_out_ref, ...), custom_call_target="tpu_custom_call" | custom-call | tf_op jit(solution)/shard_map/pallas_call | solution.py:472
Async XLA Ops:
  0.6 0.7 copy-start
  1.4 0.7 copy-start.1
  2.1 0.7 copy-start.2

commit v3 on v2

--- a/solution.py
+++ b/solution.py
@@ -18,11 +18,13 @@
 BLOCK = NY * NC * ROWS
 NX = 4
 GROUPS = ((0, 1), (1, 2), (3, 2), (5, 2), (7, 1))
-PLACES = ((1, 128), (0, 0), (0, 128), (1, 0), (1, 192))
-HALF = 256
-FIRST_Y = 5
+PLACES = ((1152, 128, 0), (0, 256, 0), (0, 256, 128), (768, 128, 0), (1152, 128, 64))
+ROUNDS = ((0, 768), (768, 384), (1152, 384))
+SUM_COLUMNS = 1536
+FIRST_Y = 7
 STEPS = (
-    "10a1200130a2", "11024021a312", "3103a4504122", "041332605114", "702342613352", "247143346253",
+    "x0h110a1h22001x1a230h31102x2a340h4211203a450x331220413x460b0",
+    "3241147023425133245261b1433462b2v0537172446354b3v17364b4",
 )
 FEAT, HID = 768, 384
 
@@ -129,40 +131,45 @@
     drain(xg.at[:, z, c, pl.ds(0, 3)], y_recv)
     own = xg.at[:, z, c]
     remote(own, own, c_send, c_recv.at[0], at(z, y, 1 - c), n).start()
-    remote(own, own, z_send, z_recv.at[1], at(lax.rem(z + 1, NZ), y, c), n).start()
-    remote(own, own, z_send, z_recv.at[2], at(lax.rem(z + NZ - 1, NZ), y, c), n).start()
+    for array in range(2):
+        half = xg.at[array, z, c]
+        for k in (1, 2):
+            to = at(lax.rem(z + (NZ - 1 if k == 2 else 1), NZ), y, c)
+            remote(half, half, z_send, z_recv.at[k, array], to, n).start()
 
     def block_of(k):
         return lax.rem(z + NZ + (1 - 2 * (k % 2)) * ((k + 1) // 2), NZ)
 
-    def arrive(group):
-        first, count = GROUPS[group]
-        for k in range(max(first, 1), first + count):
-            zb = block_of(k)
-            here = xg.at[:, zb, c]
-            if k < 7:
-                drain(here, z_recv.at[k])
+    def arrive(group, array):
+        first, count = GROUPS[group]
+        for k in range(first, first + count):
+            here = xg.at[array, block_of(k), c]
+            drain(here, z_recv.at[k, array])
+            if k < 5 or k - 5 == array:
                 onward = at(lax.rem(z + NZ - 1 + 2 * (k % 2), NZ), y, c)
-                passed = here if k < 5 else xg.at[k - 5, zb, c]
-                remote(passed, passed, z_send, z_recv.at[k + 2], onward, n).start()
-            else:
-                drain(xg.at[0, zb, c], z_recv.at[7])
-                drain(xg.at[1, zb, c], z_recv.at[8])
+                remote(here, here, z_send, z_recv.at[k + 2 if k < 5 else 7, array], onward, n).start()
+        for k in range(first, first + count):
+            here = xg.at[array, block_of(k), c]
             remote(here, here, c_send, c_recv.at[k], at(z, y, 1 - c), n).start()
 
+    def tokens(array, group):
+        first, count = GROUPS[group]
+        return jnp.concatenate(
+            [xg[array, block_of(k)].reshape(BLOCK, FEAT) for k in range(first, first + count)], axis=0
+        )
+
+    def hidden(which, group):
+        first, count = GROUPS[group]
+        return jnp.concatenate(
+            [ag[:, k, which].reshape(BLOCK, HID) for k in range(first, first + count)], axis=0
+        )
+
     def forward(group):
         first, count = GROUPS[group]
-        turn, start = PLACES[group]
-        size = count * BLOCK
-        blocks = [block_of(k) for k in range(first, first + count)]
-        for zb, k in zip(blocks, range(first, first + count)):
-            drain(xg.at[:, zb, 1 - c], c_recv.at[k])
-        g_rows = jnp.concatenate([xg[1, zb].reshape(BLOCK, FEAT) for zb in blocks], axis=0)
-        g_pair = split(g_rows)
-        grad_act = dot3(g_pair, w_out_h[...], w_out_l[...])
-        x_rows = jnp.concatenate([xg[0, zb].reshape(BLOCK, FEAT) for zb in blocks], axis=0)
-        x_pair = split(x_rows)
-        pre = dot3(x_pair, w_in_h[...], w_in_l[...])
+        for k in range(first, first + count):
+            drain(xg.at[:, block_of(k), 1 - c], c_recv.at[k])
+        pre = dot3(split(tokens(0, group)), w_in_h[...], w_in_l[...])
+        grad_act = dot3(split(tokens(1, group)), w_out_h[...], w_out_l[...])
         for b in range(count):
             rows = slice(b * BLOCK, (b + 1) * BLOCK)
             part[:, first + b, 0] = pre[rows].reshape(NN, ROWS, HID)
@@ -173,11 +180,15 @@
         remote(part.at[NX + far, some], relay.at[1, some], f_send, f_recv.at[group], wide, to_left).start()
         remote(part.at[NX + right, some], near.at[0, 1, some], n_send, n_recv.at[group], wide, to_right).start()
         remote(part.at[left, some], near.at[1, 0, some], n_send, n_recv.at[group], wide, to_left).start()
-        across = split(x_rows.T)
-        for third, which in enumerate((0, 1, 0)):
-            x_across[turn, :, HALF * third + start:HALF * third + start + size] = across[which]
-        for third, which in enumerate((0, 0, 1)):
-            g_along[turn, HALF * third + start:HALF * third + start + size, :] = g_pair[which]
+
+    def keep_tokens(group):
+        column, third, start = PLACES[group]
+        size = GROUPS[group][1] * BLOCK
+        across, along = split(tokens(0, group).T), split(tokens(1, group))
+        for i in range(3):
+            place = slice(column + third * i + start, column + third * i + start + size)
+            x_across[:, place] = across[(0, 1, 0)[i]]
+            g_along[place, :] = along[(0, 0, 1)[i]]
 
     def pass_on(group):
         some = pl.ds(*GROUPS[group])
@@ -233,28 +244,24 @@
 
     def backward(group):
         first, count = GROUPS[group]
-        turn, start = PLACES[group]
-        size = count * BLOCK
-        drain(ag.at[pl.ds(0, 2), pl.ds(first, count)], a_far_recv.at[group])
-        grad_pre = jnp.concatenate(
-            [ag[:, k, 1].reshape(BLOCK, HID) for k in range(first, first + count)], axis=0
-        )
-        pair = split(grad_pre)
-        grad = dot3(pair, w_back_h[...], w_back_l[...])
-        gi[pl.ds(first, count)] = grad.reshape(count, NC, NY, ROWS, FEAT)
         some = pl.ds(first, count)
+        drain(ag.at[pl.ds(0, 2), some], a_far_recv.at[group])
+        grad = dot3(split(hidden(1, group)), w_back_h[...], w_back_l[...])
+        gi[some] = grad.reshape(count, NC, NY, ROWS, FEAT)
         remote(
             gi.at[some, 1 - c], gi_core.at[some], gc_send, gc_recv.at[group], at(z, y, 1 - c), n
         ).start()
+
+    def keep_hidden(group):
+        column, third, start = PLACES[group]
+        size = GROUPS[group][1] * BLOCK
+        grad_pre = hidden(1, group)
         bias[...] += jnp.sum(grad_pre.reshape(size // 8, 8, HID), axis=0)
-        act = jnp.concatenate(
-            [ag[:, k, 0].reshape(BLOCK, HID) for k in range(first, first + count)], axis=0
-        )
-        across = split(act.T)
-        for third, which in enumerate((0, 1, 0)):
-            a_across[turn, :, HALF * third + start:HALF * third + start + size] = across[which]
-        for third, which in enumerate((0, 0, 1)):
-            p_along[turn, HALF * third + start:HALF * third + start + size, :] = pair[which]
+        across, along = split(hidden(0, group).T), split(grad_pre)
+        for i in range(3):
+            place = slice(column + third * i + start, column + third * i + start + size)
+            a_across[:, place] = across[(0, 1, 0)[i]]
+            p_along[place, :] = along[(0, 0, 1)[i]]
 
     def hand_over(group):
         first, count = GROUPS[group]
@@ -271,12 +278,12 @@
                 remote(
                     gi.at[pl.ds(first, count), c, to],
                     gi_y_first.at[j - 1, pl.ds(first - FIRST_Y, count)],
-                    gyf_send, gyf_recv.at[group - 3], at(z, to, c), n,
+                    gyf_send, gyf_recv, at(z, to, c), n,
                 ).start()
 
     def to_owner(group):
         first, count = GROUPS[group]
-        drain(gi_y_first.at[:, pl.ds(first - FIRST_Y, count)], gyf_recv.at[group - 3])
+        drain(gi_y_first, gyf_recv)
         for k in range(first, first + count):
             i = k - FIRST_Y
             gi[k, c, y] += gi_y_first[0, i] + (gi_y_first[1, i] + gi_y_first[2, i])
@@ -293,37 +300,34 @@
         return out
 
     def weight_round(turn, size, across, along, raw):
+        place = slice(ROUNDS[turn][0], sum(ROUNDS[turn]))
         total = jnp.zeros((8, 128), F32)
         for start in range(0, raw.shape[0], size):
             rows = slice(start, start + size)
-            tile = product(across[turn, rows, :], along[turn])
-            if turn == 1:
+            tile = product(across[rows, place], along[place, :])
+            if turn > 0:
                 tile = tile + raw[rows, :]
+            if turn == 2:
                 total = total + to_vreg(tile * tile)
             raw[rows, :] = tile
         return total
 
+    def weights(turn):
+        total = weight_round(turn, 256, x_across, p_along, raw_in_ref)
+        return total + weight_round(turn, 128, a_across, g_along, raw_out_ref)
+
     bias[...] = jnp.zeros_like(bias)
     stages = {
-        "a": arrive, "0": forward, "1": pass_on, "2": add_x, "3": activate, "4": spread,
-        "5": spread_far, "6": backward, "7": hand_over, "8": to_owner,
+        "h": lambda group: arrive(group, 0), "a": lambda group: arrive(group, 1),
+        "0": forward, "1": pass_on, "2": add_x, "3": activate, "4": spread, "5": spread_far,
+        "6": backward, "7": hand_over, "x": keep_tokens, "b": keep_hidden, "v": weights,
     }
-
-    def run(order):
-        for stage, group in zip(order[::2], order[1::2]):
-            stages[stage](int(group))
-
-    run("00")
+    forward(0)
     w_back_h[...], w_back_l[...] = split(w_in_f[...].T)
     for order in STEPS:
-        run(order)
-    weight_round(0, 256, x_across, p_along, raw_in_ref)
-    run("4463725473")
-    weight_round(0, 128, a_across, g_along, raw_out_ref)
-    run("6483")
-    total = weight_round(1, 256, x_across, p_along, raw_in_ref)
-    run("74")
-    total = total + weight_round(1, 128, a_across, g_along, raw_out_ref)
+        for stage, which in zip(order[::2], order[1::2]):
+            stages[stage](int(which))
+    total = weights(2)
 
     def share(phase, place, value, peers):
         sums[phase, place] = value
@@ -337,6 +341,11 @@
 
     share(0, n, total, [(wide, lax.rem(n + j, NN)) for j in range(1, 8)])
 
+    hand_over(4)
+    total = collect(0)
+    share(1, plane, total, [
+        (z * NY * NC + lax.rem(plane + j, NY * NC), n) for j in range(1, 8)
+    ])
     to_owner(4)
     drain(gi_z, gz_recv)
     own_sum = gi[0, c]
@@ -346,11 +355,6 @@
     for j in (2, 1, 3):
         to = lax.rem(y + j, NY)
         remote(gi.at[0, c, to], gi_y.at[j - 1], gy_send, gy_recv, at(z, to, c), n).start()
-
-    total = collect(0)
-    share(1, plane, total, [
-        (z * NY * NC + lax.rem(plane + j, NY * NC), n) for j in range(1, 8)
-    ])
     bias_in_ref[...] = jnp.sum(bias[...], axis=0, keepdims=True)
     bias_out_ref[...] = jnp.sum(xg[1].reshape(TOKENS, FEAT), axis=0, keepdims=True)
     total = collect(1)
@@ -359,9 +363,7 @@
     ])
     drain(gi_y, gy_recv)
     drain(gi_z_last, gzl_recv)
-    grad_in_ref[...] = ((gi[0, c, y] + gi_y[0]) + (gi_y[1] + gi_y[2])) + (
-        (gi_z_last[0] + gi_z_last[1]) + gi_z_last[2]
-    )
+    grad_in_ref[...] = ((gi[0, c, y] + gi_y[0]) + (gi_y[1] + gi_y[2])) + gi_z_last[0]
     drain(xg.at[:, z, c, pl.ds(0, 3)], y_send)
     drain(xg.at[:, pl.ds(0, 7), 0], z_send)
     drain(xg.at[:, :, 0], c_send)
@@ -444,15 +446,15 @@
             pltpu.VMEM((FEAT, HID), BF16),
             pltpu.VMEM((HID, FEAT), BF16),
             pltpu.VMEM((HID, FEAT), BF16),
-            pltpu.VMEM((2, FEAT, 3 * HALF), BF16),
-            pltpu.VMEM((2, 3 * HALF, FEAT), BF16),
-            pltpu.VMEM((2, 3 * HALF, HID), BF16),
-            pltpu.VMEM((2, HID, 3 * HALF), BF16),
+            pltpu.VMEM((FEAT, SUM_COLUMNS), BF16),
+            pltpu.VMEM((SUM_COLUMNS, FEAT), BF16),
+            pltpu.VMEM((SUM_COLUMNS, HID), BF16),
+            pltpu.VMEM((HID, SUM_COLUMNS), BF16),
             pltpu.VMEM((ROWS, HID), F32),
             pltpu.VMEM((HID,), F32),
             dma((5,)),
             dma, dma,
-            dma, dma((9,)),
+            dma, dma((NZ, 2)),
             dma, dma((NZ,)),
             dma, dma((5,)),
             dma, dma((5,)),
@@ -461,7 +463,7 @@
             dma, dma((5,)),
             dma, dma,
             dma, dma,
-            dma, dma((2,)),
+            dma, dma,
             dma, dma,
             dma, dma((3,)),
         ],

time: 95 us -> 87.9 us (0.925)
  Pallas kernels: 91.9 us -> 84.9 us
    pallas_call x1, Pallas kernels: 89.8 us -> 82.8 us  [local(): pl.pallas_call(kernel, out_shape=(jax.ShapeDtypeStruct((ROWS, FEAT), F32)...]
where the time goes in v3:
time: 87.9 us; the launch traced here: 87.7 us
  Pallas kernels  84.9 us (97%)
  local copies, waits for them, and re-layouts  2.15 us (2%)
    pallas_call x1, Pallas kernels, local(): pl.pallas_call(kernel, out_shape=(jax.ShapeDtypeStruct((ROWS, FEAT), F32)...  82.8 us
    unnamed x6, local copies, waits for them, and re-layouts  2.15 us
    pallas_call x1, Pallas kernels, local(): pl.pallas_call(scale_kernel, out_shape=(jax.ShapeDtypeStruct((ROWS, FEAT)...  2.12 us

profile of v3, /device:TPU:1, one launch (start us, length us, event | category | flops | bytes accessed | tf_op | source)
XLA Modules:
  0.0 87.7 jit_solution(13255341800525496225)
XLA Ops:
  0.6 0.0 copy-start
  0.6 0.7 copy-done
  1.4 0.0 copy-start.1
  1.4 0.7 copy-done.1
  2.1 0.0 copy-start.2
  2.1 0.7 copy-done.2
  2.8 82.8 %shard_map.92 = (f32[8,768]{1,0:T(8,128)S(1)}, f32[768,384]{1,0:T(8,128)S(1)}, f32[384,768]{1,0:T(8,128)S(1)}, f32[1,384]{1,0:T(1,128)S(1)}, f32[1,768]{1,0:T(1,128)S(1)}, /*index=5*/f32[8,128]{1,0:T(8,128)S(1)}) custom-call(f32[8,768]{1,0:T(8,128)S(1)} %copy-done, f32[8,768]{1,0:T(8,128)S(1)} %copy-done.1, f32[768,384]{1,0:T(8,128)} %w_in_ref.1, ...), custom_call_target="tpu_custom_call" | custom-call | tf_op jit(solution)/shard_map/pallas_call | solution.py:415
  85.6 2.1 %shard_map.93 = (f32[8,768]{1,0:T(8,128)}, f32[768,384]{1,0:T(8,128)}, f32[384,768]{1,0:T(8,128)}, f32[384]{0:T(512)}, f32[768]{0:T(1024)}) custom-call(f32[8,768]{1,0:T(8,128)S(1)} %get-tuple-element.11.grad_in_ref, f32[768,384]{1,0:T(8,128)S(1)} %get-tuple-element.12.raw_in_ref, f32[384,768]{1,0:T(8,128)S(1)} %get-tuple-element.13.raw_out_ref, ...), custom_call_target="tpu_custom_call" | custom-call | tf_op jit(solution)/shard_map/pallas_call | solution.py:474
Async XLA Ops:
  0.6 0.7 copy-start
  1.4 0.7 copy-start.1
  2.1 0.7 copy-start.2

commit v4 on v3

--- a/solution.py
+++ b/solution.py
@@ -23,8 +23,8 @@
 SUM_COLUMNS = 1536
 FIRST_Y = 7
 STEPS = (
-    "x0h110a1h22001x1a230h31102x2a340h4211203a450x331220413x460b0",
-    "3241147023425133245261b1433462b2v0537172446354b3v17364b4",
+    "x0h1a11001x1h230a211h30240x231a3h41203a460b0x3410470",
+    "32x41361b1147142333462b2v043724463b3v17364b4",
 )
 FEAT, HID = 768, 384
 
@@ -75,11 +75,11 @@
 def kernel(
     x_ref, g_ref, w_in_ref, b_ref, w_out_ref,
     grad_in_ref, raw_in_ref, raw_out_ref, bias_in_ref, bias_out_ref, factor_ref,
-    xg, part, relay, near, across_y, ag, gi, gi_core, gi_z, gi_y, gi_y_first, gi_z_last, sums,
+    xg, part, relay, near, ag, gi, gi_core, gi_z, gi_y, gi_y_first, gi_z_last, sums,
     w_in_f, w_out_f, w_in_h, w_in_l, w_out_h, w_out_l, w_back_h, w_back_l,
     x_across, g_along, p_along, a_across, bias, b_here,
     load_sem, y_send, y_recv, z_send, z_recv, c_send, c_recv,
-    f_send, f_recv, n_send, n_recv, s_y_send, s_y_recv, a_send, a_y_recv, a_one_recv, a_two_recv, a_far_recv,
+    f_send, f_recv, n_send, n_recv, a_send, a_one_recv, a_far_recv,
     gc_send, gc_recv, gz_send, gz_recv, gy_send, gy_recv, gyf_send, gyf_recv, gzl_send, gzl_recv,
     s_send, s_recv,
 ):
@@ -118,24 +118,30 @@
     load_g.wait()
     pl.semaphore_wait(barrier, 21)
 
-    for j in (2, 1, 3):
-        own = xg.at[:, z, c, y]
-        remote(own, own, y_send, y_recv, at(z, lax.rem(y + j, NY), c), n).start()
-
+    def first_row(row):
+        part_of = xg.at[:, z, c, row]
+        for k in (1, 2):
+            to = at(lax.rem(z + (NZ - 1 if k == 2 else 1), NZ), y, c)
+            remote(part_of, part_of, z_send, z_recv.at[k, 0], to, n).start()
+        remote(part_of, part_of, c_send, c_recv.at[0], at(z, y, 1 - c), n).start()
+
+    def next_row(j):
+        row = lax.rem(y + NY - j, NY)
+        drain(xg.at[:, z, c, row], y_recv.at[j - 1])
+        first_row(row)
+
+    own = xg.at[:, z, c, y]
+    for j in (1, 3, 2):
+        remote(own, own, y_send, y_recv.at[j - 1], at(z, lax.rem(y + j, NY), c), n).start()
+    first_row(y)
     load_in.wait()
     w_in_h[...], w_in_l[...] = split(w_in_f[...])
+    next_row(1)
+    next_row(3)
     load_out.wait()
     w_out_h[...], w_out_l[...] = split(w_out_f[...].T)
     load_b.wait()
-
-    drain(xg.at[:, z, c, pl.ds(0, 3)], y_recv)
-    own = xg.at[:, z, c]
-    remote(own, own, c_send, c_recv.at[0], at(z, y, 1 - c), n).start()
-    for array in range(2):
-        half = xg.at[array, z, c]
-        for k in (1, 2):
-            to = at(lax.rem(z + (NZ - 1 if k == 2 else 1), NZ), y, c)
-            remote(half, half, z_send, z_recv.at[k, array], to, n).start()
+    next_row(2)
 
     def block_of(k):
         return lax.rem(z + NZ + (1 - 2 * (k % 2)) * ((k + 1) // 2), NZ)
@@ -144,7 +150,10 @@
         first, count = GROUPS[group]
         for k in range(first, first + count):
             here = xg.at[array, block_of(k), c]
-            drain(here, z_recv.at[k, array])
+            if group > 1:
+                drain(here, z_recv.at[k, array])
+            elif array == 0:
+                drain(xg.at[:, block_of(k), c], z_recv.at[k, 0])
             if k < 5 or k - 5 == array:
                 onward = at(lax.rem(z + NZ - 1 + 2 * (k % 2), NZ), y, c)
                 remote(here, here, z_send, z_recv.at[k + 2 if k < 5 else 7, array], onward, n).start()
@@ -178,8 +187,8 @@
         to_right, to_left = yl * NX + right, yl * NX + left
         remote(part.at[far, some], relay.at[0, some], f_send, f_recv.at[group], wide, to_right).start()
         remote(part.at[NX + far, some], relay.at[1, some], f_send, f_recv.at[group], wide, to_left).start()
-        remote(part.at[NX + right, some], near.at[0, 1, some], n_send, n_recv.at[group], wide, to_right).start()
-        remote(part.at[left, some], near.at[1, 0, some], n_send, n_recv.at[group], wide, to_left).start()
+        for owner, slot in ((NX + right, 3 - 2 * yl), (left, 2 + 2 * yl), (over, 0)):
+            remote(part.at[owner, some], near.at[slot, some], n_send, n_recv.at[group], wide, owner).start()
 
     def keep_tokens(group):
         column, third, start = PLACES[group]
@@ -195,52 +204,28 @@
         drain(relay.at[:, some], f_recv.at[group])
         part[right, some] += relay[0, some]
         part[NX + left, some] += relay[1, some]
-        remote(
-            part.at[right, some], near.at[0, 0, some], n_send, n_recv.at[group], wide, yl * NX + right
-        ).start()
-        remote(
-            part.at[NX + left, some], near.at[1, 1, some], n_send, n_recv.at[group], wide, yl * NX + left
-        ).start()
-
-    def add_x(group):
-        some = pl.ds(*GROUPS[group])
-        drain(near.at[:, :, some], n_recv.at[group])
-        part[over, some] += near[0, 1 - yl, some] + near[1, 1 - yl, some]
-        remote(
-            part.at[over, some], across_y.at[some], s_y_send, s_y_recv.at[group], wide, over
-        ).start()
-        part[n, some] += near[0, yl, some] + near[1, yl, some]
+        for owner, slot in ((right, 1 + 2 * yl), (NX + left, 4 - 2 * yl)):
+            remote(part.at[owner, some], near.at[slot, some], n_send, n_recv.at[group], wide, owner).start()
 
     def activate(group):
         some = pl.ds(*GROUPS[group])
-        drain(across_y.at[some], s_y_recv.at[group])
-        total = part[n, some] + across_y[some]
+        drain(near.at[:, some], n_recv.at[group])
+        total = part[n, some]
+        for j in range(5):
+            total = total + near[j, some]
         act, slope = gelu_parts(total[:, 0] + b_here[...])
         ag[n, some, 0] = act
         ag[n, some, 1] = total[:, 1] * slope
         mine = ag.at[n, some]
-        remote(mine, mine, a_send, a_y_recv.at[group], wide, over).start()
-        for side in (right, left):
-            remote(mine, mine, a_send, a_one_recv.at[group], wide, yl * NX + side).start()
-
-    ahead = lax.rem(x + 1 + 2 * yl, NX)
-    behind = lax.rem(x + 3 - 2 * yl, NX)
+        for peer in (right, NX + right, left, NX + left, over):
+            remote(mine, mine, a_send, a_one_recv.at[group], wide, peer).start()
 
     def spread(group):
         some = pl.ds(*GROUPS[group])
-        drain(across_y.at[some], a_y_recv.at[group])
-        other = ag.at[over, some]
-        for side in (right, left):
-            remote(other, other, a_send, a_two_recv.at[group], wide, yl * NX + side).start()
-        drain(ag.at[pl.ds(0, 2), some], a_one_recv.at[group])
-        chunk = ag.at[yl * NX + behind, some]
-        remote(chunk, chunk, a_send, a_far_recv.at[group], wide, yl * NX + ahead).start()
-
-    def spread_far(group):
-        some = pl.ds(*GROUPS[group])
-        drain(ag.at[pl.ds(0, 2), some], a_two_recv.at[group])
-        chunk = ag.at[(1 - yl) * NX + ahead, some]
-        remote(chunk, chunk, a_send, a_far_recv.at[group], wide, yl * NX + behind).start()
+        drain(ag.at[pl.ds(0, 5), some], a_one_recv.at[group])
+        for owner, peer in ((left, yl * NX + right), (NX + right, yl * NX + left)):
+            chunk = ag.at[owner, some]
+            remote(chunk, chunk, a_send, a_far_recv.at[group], wide, peer).start()
 
     def backward(group):
         first, count = GROUPS[group]
@@ -319,7 +304,7 @@
     bias[...] = jnp.zeros_like(bias)
     stages = {
         "h": lambda group: arrive(group, 0), "a": lambda group: arrive(group, 1),
-        "0": forward, "1": pass_on, "2": add_x, "3": activate, "4": spread, "5": spread_far,
+        "0": forward, "1": pass_on, "3": activate, "4": spread,
         "6": backward, "7": hand_over, "x": keep_tokens, "b": keep_hidden, "v": weights,
     }
     forward(0)
@@ -369,7 +354,6 @@
     drain(xg.at[:, :, 0], c_send)
     drain(relay, f_send)
     drain(near, n_send)
-    drain(across_y, s_y_send)
     drain(ag.at[pl.ds(0, 7)], a_send)
     drain(gi_core, gc_send)
     drain(gi_z, gz_send)
@@ -428,8 +412,7 @@
             pltpu.VMEM((2, NZ, NC, NY, ROWS, FEAT), F32),
             pltpu.VMEM((NN, NZ, 2, ROWS, HID), F32),
             pltpu.VMEM((2, NZ, 2, ROWS, HID), F32),
-            pltpu.VMEM((2, 2, NZ, 2, ROWS, HID), F32),
-            pltpu.VMEM((NZ, 2, ROWS, HID), F32),
+            pltpu.VMEM((5, NZ, 2, ROWS, HID), F32),
             pltpu.VMEM((NN, NZ, 2, ROWS, HID), F32),
             pltpu.VMEM((NZ, NC, NY, ROWS, FEAT), F32),
             pltpu.VMEM((NZ, NY, ROWS, FEAT), F32),
@@ -453,13 +436,12 @@
             pltpu.VMEM((ROWS, HID), F32),
             pltpu.VMEM((HID,), F32),
             dma((5,)),
-            dma, dma,
+            dma, dma((NY - 1,)),
             dma, dma((NZ, 2)),
             dma, dma((NZ,)),
             dma, dma((5,)),
             dma, dma((5,)),
-            dma, dma((5,)),
-            dma, dma((5,)), dma((5,)), dma((5,)), dma((5,)),
+            dma, dma((5,)), dma((5,)),
             dma, dma((5,)),
             dma, dma,
             dma, dma,

time: 87.9 us -> 83.9 us (0.954)
  Pallas kernels: 84.9 us -> 80.8 us
    pallas_call x1, Pallas kernels: 82.8 us -> 78.7 us  [local(): pl.pallas_call(kernel, out_shape=(jax.ShapeDtypeStruct((ROWS, FEAT), F32)...]
where the time goes in v4:
time: 83.9 us; the launch traced here: 83.6 us
  Pallas kernels  80.8 us (96%)
  local copies, waits for them, and re-layouts  2.15 us (3%)
    pallas_call x1, Pallas kernels, local(): pl.pallas_call(kernel, out_shape=(jax.ShapeDtypeStruct((ROWS, FEAT), F32)...  78.7 us
    unnamed x6, local copies, waits for them, and re-layouts  2.15 us
    pallas_call x1, Pallas kernels, local(): pl.pallas_call(scale_kernel, out_shape=(jax.ShapeDtypeStruct((ROWS, FEAT)...  2.12 us

profile of v4, /device:TPU:1, one launch (start us, length us, event | category | flops | bytes accessed | tf_op | source)
XLA Modules:
  0.0 83.6 jit_solution(7561410251116319033)
XLA Ops:
  0.6 0.0 copy-start
  0.6 0.7 copy-done
  1.4 0.0 copy-start.1
  1.4 0.7 copy-done.1
  2.1 0.0 copy-start.2
  2.1 0.7 copy-done.2
  2.8 78.7 %shard_map.92 = (f32[8,768]{1,0:T(8,128)S(1)}, f32[768,384]{1,0:T(8,128)S(1)}, f32[384,768]{1,0:T(8,128)S(1)}, f32[1,384]{1,0:T(1,128)S(1)}, f32[1,768]{1,0:T(1,128)S(1)}, /*index=5*/f32[8,128]{1,0:T(8,128)S(1)}) custom-call(f32[8,768]{1,0:T(8,128)S(1)} %copy-done, f32[8,768]{1,0:T(8,128)S(1)} %copy-done.1, f32[768,384]{1,0:T(8,128)} %w_in_ref.1, ...), custom_call_target="tpu_custom_call" | custom-call | tf_op jit(solution)/shard_map/pallas_call | solution.py:399
  81.5 2.1 %shard_map.93 = (f32[8,768]{1,0:T(8,128)}, f32[768,384]{1,0:T(8,128)}, f32[384,768]{1,0:T(8,128)}, f32[384]{0:T(512)}, f32[768]{0:T(1024)}) custom-call(f32[8,768]{1,0:T(8,128)S(1)} %get-tuple-element.11.grad_in_ref, f32[768,384]{1,0:T(8,128)S(1)} %get-tuple-element.12.raw_in_ref, f32[384,768]{1,0:T(8,128)S(1)} %get-tuple-element.13.raw_out_ref, ...), custom_call_target="tpu_custom_call" | custom-call | tf_op jit(solution)/shard_map/pallas_call | solution.py:456
Async XLA Ops:
  0.6 0.7 copy-start
  1.4 0.7 copy-start.1
  2.1 0.7 copy-start.2

commit v5 on v4

--- a/solution.py
+++ b/solution.py
@@ -21,10 +21,10 @@
 PLACES = ((1152, 128, 0), (0, 256, 0), (0, 256, 128), (768, 128, 0), (1152, 128, 64))
 ROUNDS = ((0, 768), (768, 384), (1152, 384))
 SUM_COLUMNS = 1536
-FIRST_Y = 7
+FIRST_Y = 5
 STEPS = (
-    "x0h1a11001x1h230a211h30240x231a3h41203a460b0x3410470",
-    "32x41361b1147142333462b2v043724463b3v17364b4",
+    "x0h1a11001x1h230a211h30240x231a3h41203a460x3b0410470",
+    "x413326114b1337142346243b2v044v17263b364w0w173b474u0u1",
 )
 FEAT, HID = 768, 384
 
@@ -263,12 +263,12 @@
                 remote(
                     gi.at[pl.ds(first, count), c, to],
                     gi_y_first.at[j - 1, pl.ds(first - FIRST_Y, count)],
-                    gyf_send, gyf_recv, at(z, to, c), n,
+                    gyf_send, gyf_recv.at[group - 3], at(z, to, c), n,
                 ).start()
 
     def to_owner(group):
         first, count = GROUPS[group]
-        drain(gi_y_first, gyf_recv)
+        drain(gi_y_first.at[:, pl.ds(first - FIRST_Y, count)], gyf_recv.at[group - 3])
         for k in range(first, first + count):
             i = k - FIRST_Y
             gi[k, c, y] += gi_y_first[0, i] + (gi_y_first[1, i] + gi_y_first[2, i])
@@ -297,22 +297,32 @@
             raw[rows, :] = tile
         return total
 
+    totals = []
+
     def weights(turn):
-        total = weight_round(turn, 256, x_across, p_along, raw_in_ref)
-        return total + weight_round(turn, 128, a_across, g_along, raw_out_ref)
+        def one(which):
+            if which == 0:
+                total = weight_round(turn, 256, x_across, p_along, raw_in_ref)
+            else:
+                total = weight_round(turn, 128, a_across, g_along, raw_out_ref)
+            if turn == 2:
+                totals.append(total)
+
+        return one
 
     bias[...] = jnp.zeros_like(bias)
     stages = {
         "h": lambda group: arrive(group, 0), "a": lambda group: arrive(group, 1),
         "0": forward, "1": pass_on, "3": activate, "4": spread,
-        "6": backward, "7": hand_over, "x": keep_tokens, "b": keep_hidden, "v": weights,
+        "6": backward, "7": hand_over, "x": keep_tokens, "b": keep_hidden,
+        "v": weights(0), "w": weights(1), "u": weights(2),
     }
     forward(0)
     w_back_h[...], w_back_l[...] = split(w_in_f[...].T)
     for order in STEPS:
         for stage, which in zip(order[::2], order[1::2]):
             stages[stage](int(which))
-    total = weights(2)
+    total = totals[0] + totals[1]
 
     def share(phase, place, value, peers):
         sums[phase, place] = value
@@ -326,12 +336,6 @@
 
     share(0, n, total, [(wide, lax.rem(n + j, NN)) for j in range(1, 8)])
 
-    hand_over(4)
-    total = collect(0)
-    share(1, plane, total, [
-        (z * NY * NC + lax.rem(plane + j, NY * NC), n) for j in range(1, 8)
-    ])
-    to_owner(4)
     drain(gi_z, gz_recv)
     own_sum = gi[0, c]
     for j in range(FIRST_Y - 1):
@@ -340,15 +344,23 @@
     for j in (2, 1, 3):
         to = lax.rem(y + j, NY)
         remote(gi.at[0, c, to], gi_y.at[j - 1], gy_send, gy_recv, at(z, to, c), n).start()
+    total = collect(0)
+    share(1, plane, total, [
+        (z * NY * NC + lax.rem(plane + j, NY * NC), n) for j in range(1, 8)
+    ])
     bias_in_ref[...] = jnp.sum(bias[...], axis=0, keepdims=True)
     bias_out_ref[...] = jnp.sum(xg[1].reshape(TOKENS, FEAT), axis=0, keepdims=True)
+    to_owner(3)
     total = collect(1)
     share(2, z, total, [
         (lax.rem(z + j, NZ) * NY * NC + plane, n) for j in range(1, 8)
     ])
+    to_owner(4)
     drain(gi_y, gy_recv)
     drain(gi_z_last, gzl_recv)
-    grad_in_ref[...] = ((gi[0, c, y] + gi_y[0]) + (gi_y[1] + gi_y[2])) + gi_z_last[0]
+    grad_in_ref[...] = ((gi[0, c, y] + gi_y[0]) + (gi_y[1] + gi_y[2])) + (
+        (gi_z_last[0] + gi_z_last[1]) + gi_z_last[2]
+    )
     drain(xg.at[:, z, c, pl.ds(0, 3)], y_send)
     drain(xg.at[:, pl.ds(0, 7), 0], z_send)
     drain(xg.at[:, :, 0], c_send)
@@ -445,7 +457,7 @@
             dma, dma((5,)),
             dma, dma,
             dma, dma,
-            dma, dma,
+            dma, dma((2,)),
             dma, dma,
             dma, dma((3,)),
         ],

time: 83.9 us -> 88.4 us (1.054)
  Pallas kernels: 80.8 us -> 85.3 us
    pallas_call x1, Pallas kernels: 78.7 us -> 83.2 us  [local(): pl.pallas_call(kernel, out_shape=(jax.ShapeDtypeStruct((ROWS, FEAT), F32)...]
where the time goes in v5:
time: 88.4 us; the launch traced here: 88.1 us
  Pallas kernels  85.3 us (96%)
  local copies, waits for them, and re-layouts  2.15 us (2%)
    pallas_call x1, Pallas kernels, local(): pl.pallas_call(kernel, out_shape=(jax.ShapeDtypeStruct((ROWS, FEAT), F32)...  83.2 us
    unnamed x6, local copies, waits for them, and re-layouts  2.15 us
    pallas_call x1, Pallas kernels, local(): pl.pallas_call(scale_kernel, out_shape=(jax.ShapeDtypeStruct((ROWS, FEAT)...  2.12 us

profile of v5, /device:TPU:1, one launch (start us, length us, event | category | flops | bytes accessed | tf_op | source)
XLA Modules:
  0.0 88.1 jit_solution(17866506397993170073)
XLA Ops:
  0.6 0.0 copy-start
  0.6 0.7 copy-done
  1.4 0.0 copy-start.1
  1.4 0.7 copy-done.1
  2.1 0.0 copy-start.2
  2.1 0.7 copy-done.2
  2.8 83.2 %shard_map.92 = (f32[8,768]{1,0:T(8,128)S(1)}, f32[768,384]{1,0:T(8,128)S(1)}, f32[384,768]{1,0:T(8,128)S(1)}, f32[1,384]{1,0:T(1,128)S(1)}, f32[1,768]{1,0:T(1,128)S(1)}, /*index=5*/f32[8,128]{1,0:T(8,128)S(1)}) custom-call(f32[8,768]{1,0:T(8,128)S(1)} %copy-done, f32[8,768]{1,0:T(8,128)S(1)} %copy-done.1, f32[768,384]{1,0:T(8,128)} %w_in_ref.1, ...), custom_call_target="tpu_custom_call" | custom-call | tf_op jit(solution)/shard_map/pallas_call | solution.py:411
  86.0 2.1 %shard_map.93 = (f32[8,768]{1,0:T(8,128)}, f32[768,384]{1,0:T(8,128)}, f32[384,768]{1,0:T(8,128)}, f32[384]{0:T(512)}, f32[768]{0:T(1024)}) custom-call(f32[8,768]{1,0:T(8,128)S(1)} %get-tuple-element.11.grad_in_ref, f32[768,384]{1,0:T(8,128)S(1)} %get-tuple-element.12.raw_in_ref, f32[384,768]{1,0:T(8,128)S(1)} %get-tuple-element.13.raw_out_ref, ...), custom_call_target="tpu_custom_call" | custom-call | tf_op jit(solution)/shard_map/pallas_call | solution.py:468
Async XLA Ops:
  0.6 0.7 copy-start
  1.4 0.7 copy-start.1
  2.1 0.7 copy-start.2

commit v6 on v4

--- a/solution.py
+++ b/solution.py
@@ -24,7 +24,7 @@
 FIRST_Y = 7
 STEPS = (
     "x0h1a11001x1h230a211h30240x231a3h41203a460b0x3410470",
-    "32x41361b1147142333462b2v043724463b3v17364b4",
+    "32x41361b1147142333462b2v043v1724463b3w073w164b4u0u1",
 )
 FEAT, HID = 768, 384
 
@@ -297,22 +297,32 @@
             raw[rows, :] = tile
         return total
 
+    totals = []
+
     def weights(turn):
-        total = weight_round(turn, 256, x_across, p_along, raw_in_ref)
-        return total + weight_round(turn, 128, a_across, g_along, raw_out_ref)
+        def one(which):
+            if which == 0:
+                total = weight_round(turn, 256, x_across, p_along, raw_in_ref)
+            else:
+                total = weight_round(turn, 128, a_across, g_along, raw_out_ref)
+            if turn == 2:
+                totals.append(total)
+
+        return one
 
     bias[...] = jnp.zeros_like(bias)
     stages = {
         "h": lambda group: arrive(group, 0), "a": lambda group: arrive(group, 1),
         "0": forward, "1": pass_on, "3": activate, "4": spread,
-        "6": backward, "7": hand_over, "x": keep_tokens, "b": keep_hidden, "v": weights,
+        "6": backward, "7": hand_over, "x": keep_tokens, "b": keep_hidden,
+        "v": weights(0), "w": weights(1), "u": weights(2),
     }
     forward(0)
     w_back_h[...], w_back_l[...] = split(w_in_f[...].T)
     for order in STEPS:
         for stage, which in zip(order[::2], order[1::2]):
             stages[stage](int(which))
-    total = weights(2)
+    total = totals[0] + totals[1]
 
     def share(phase, place, value, peers):
         sums[phase, place] = value
@@ -452,7 +462,7 @@
         compiler_params=pltpu.CompilerParams(
             collective_id=0, has_side_effects=True, vmem_limit_bytes=51 * 1024 * 1024
         ),
-    )(x_tokens, grad_out, w_in, b_in, w_out)
+    )(*(pltpu.with_memory_space_constraint(a, pltpu.HBM) for a in (x_tokens, grad_out, w_in, b_in, w_out)))
     return pl.pallas_call(
         scale_kernel,
         out_shape=(

time: 83.9 us -> 81.6 us (0.973)
  local copies, waits for them, and re-layouts: 2.15 us -> 0 us
    unnamed x6 -> x0, local copies, waits for them, and re-layouts: 2.15 us -> none
where the time goes in v6:
time: 81.6 us; the launch traced here: 81.4 us
  Pallas kernels  80.8 us (99%)
    pallas_call x1, Pallas kernels, local(): pl.pallas_call(kernel, out_shape=(jax.ShapeDtypeStruct((ROWS, FEAT), F32)...  78.7 us
    pallas_call x1, Pallas kernels, local(): pl.pallas_call(scale_kernel, out_shape=(jax.ShapeDtypeStruct((ROWS, FEAT)...  2.12 us

profile of v6, /device:TPU:1, one launch (start us, length us, event | category | flops | bytes accessed | tf_op | source)
XLA Modules:
  0.0 81.4 jit_solution(11888978168741351581)
XLA Ops:
  0.6 78.7 %shard_map.92 = (f32[8,768]{1,0:T(8,128)S(1)}, f32[768,384]{1,0:T(8,128)S(1)}, f32[384,768]{1,0:T(8,128)S(1)}, f32[1,384]{1,0:T(1,128)S(1)}, f32[1,768]{1,0:T(1,128)S(1)}, /*index=5*/f32[8,128]{1,0:T(8,128)S(1)}) custom-call(f32[8,768]{1,0:T(8,128)} %x_ref.1, f32[8,768]{1,0:T(8,128)} %g_ref.1, f32[768,384]{1,0:T(8,128)} %w_in_ref.1, f32[384]{0:T(512)} %b_ref.1, ...), custom_call_target="tpu_custom_call" | custom-call | tf_op jit(solution)/shard_map/pallas_call | solution.py:409
  79.3 2.1 %shard_map.93 = (f32[8,768]{1,0:T(8,128)}, f32[768,384]{1,0:T(8,128)}, f32[384,768]{1,0:T(8,128)}, f32[384]{0:T(512)}, f32[768]{0:T(1024)}) custom-call(f32[8,768]{1,0:T(8,128)S(1)} %get-tuple-element.11.grad_in_ref, f32[768,384]{1,0:T(8,128)S(1)} %get-tuple-element.12.raw_in_ref, f32[384,768]{1,0:T(8,128)S(1)} %get-tuple-element.13.raw_out_ref, ...), custom_call_target="tpu_custom_call" | custom-call | tf_op jit(solution)/shard_map/pallas_call | solution.py:466

commit v7 on v6

--- a/solution.py
+++ b/solution.py
@@ -23,8 +23,8 @@
 SUM_COLUMNS = 1536
 FIRST_Y = 7
 STEPS = (
-    "x0h1a11001x1h230a211h30240x231a3h41203a460b0x3410470",
-    "32x41361b1147142333462b2v043v1724463b3w073w164b4u0u1",
+    "x0h1a11001x1h230a211h30240x231a3h41203a460x3b0410470",
+    "x4133261b114337142346243b2v0v1724463b3w0w16473b4u0u1",
 )
 FEAT, HID = 768, 384
 
@@ -317,8 +317,8 @@
         "6": backward, "7": hand_over, "x": keep_tokens, "b": keep_hidden,
         "v": weights(0), "w": weights(1), "u": weights(2),
     }
+    w_back_h[...], w_back_l[...] = split(w_in_f[...].T)
     forward(0)
-    w_back_h[...], w_back_l[...] = split(w_in_f[...].T)
     for order in STEPS:
         for stage, which in zip(order[::2], order[1::2]):
             stages[stage](int(which))
@@ -381,10 +381,18 @@
 
 def scale_kernel(
     grad_in_ref, raw_in_ref, raw_out_ref, bias_in_ref, bias_out_ref, factor_ref,
-    grad_in_out, gw_in, gw_out, gb_in, gb_out, buf_in, buf_out, sems,
+    grad_in_out, gw_in, gw_out, gb_in, gb_out, buf_in, buf_out, bias_in, bias_out, sems, small_sems,
 ):
     factor = factor_ref[0:1, 0:1]
+    bias_in[...] = (bias_in_ref[...] * factor)[0]
+    bias_out[...] = (bias_out_ref[...] * factor)[0]
     stores = []
+    for i, (source, out) in enumerate(
+        ((grad_in_ref, grad_in_out), (bias_in, gb_in), (bias_out, gb_out))
+    ):
+        store = pltpu.make_async_copy(source, out, small_sems.at[i])
+        store.start()
+        stores.append(store)
     for which, (raw, buf, out) in enumerate(
         ((raw_in_ref, buf_in, gw_in), (raw_out_ref, buf_out, gw_out))
     ):
@@ -395,9 +403,6 @@
             store = pltpu.make_async_copy(buf.at[rows], out.at[rows], sems.at[which, i])
             store.start()
             stores.append(store)
-    grad_in_out[...] = grad_in_ref[...]
-    gb_in[...] = (bias_in_ref[...] * factor)[0]
-    gb_out[...] = (bias_out_ref[...] * factor)[0]
     for store in stores:
         store.wait()
 
@@ -473,11 +478,14 @@
             jax.ShapeDtypeStruct((FEAT,), F32),
         ),
         in_specs=[vmem, vmem, vmem, vmem, vmem, vmem],
-        out_specs=(vmem, anywhere, anywhere, vmem, vmem),
+        out_specs=(anywhere,) * 5,
         scratch_shapes=[
             pltpu.VMEM((FEAT, HID), F32),
             pltpu.VMEM((HID, FEAT), F32),
+            pltpu.VMEM((HID,), F32),
+            pltpu.VMEM((FEAT,), F32),
             dma((2, PIECES)),
+            dma((3,)),
         ],
         compiler_params=pltpu.CompilerParams(vmem_limit_bytes=16 * 1024 * 1024),
     )(grad_in, raw_in, raw_out, bias_in, bias_out, factor)

time: 81.6 us -> 80.8 us (level)
  no operation moved by 1% of the time
where the time goes in v7:
time: 80.8 us; the launch traced here: 80.7 us
  Pallas kernels  80 us (99%)
    pallas_call x1, Pallas kernels, local(): pl.pallas_call(kernel, out_shape=(jax.ShapeDtypeStruct((ROWS, FEAT), F32)...  78.5 us

profile of v7, /device:TPU:1, one launch (start us, length us, event | category | flops | bytes accessed | tf_op | source)
XLA Modules:
  0.0 80.7 jit_solution(17807347926202577999)
XLA Ops:
  0.6 78.5 %shard_map.92 = (f32[8,768]{1,0:T(8,128)S(1)}, f32[768,384]{1,0:T(8,128)S(1)}, f32[384,768]{1,0:T(8,128)S(1)}, f32[1,384]{1,0:T(1,128)S(1)}, f32[1,768]{1,0:T(1,128)S(1)}, /*index=5*/f32[8,128]{1,0:T(8,128)S(1)}) custom-call(f32[8,768]{1,0:T(8,128)} %x_ref.1, f32[8,768]{1,0:T(8,128)} %g_ref.1, f32[768,384]{1,0:T(8,128)} %w_in_ref.1, f32[384]{0:T(512)} %b_ref.1, ...), custom_call_target="tpu_custom_call" | custom-call | tf_op jit(solution)/shard_map/pallas_call | solution.py:414
  79.1 1.5 %shard_map.93 = (f32[8,768]{1,0:T(8,128)}, f32[768,384]{1,0:T(8,128)}, f32[384,768]{1,0:T(8,128)}, f32[384]{0:T(512)}, f32[768]{0:T(1024)}) custom-call(f32[8,768]{1,0:T(8,128)S(1)} %get-tuple-element.11.grad_in_ref, f32[768,384]{1,0:T(8,128)S(1)} %get-tuple-element.12.raw_in_ref, f32[384,768]{1,0:T(8,128)S(1)} %get-tuple-element.13.raw_out_ref, ...), custom_call_target="tpu_custom_call" | custom-call | tf_op jit(solution)/shard_map/pallas_call | solution.py:471

commit v8 on v7

--- a/solution.py
+++ b/solution.py
@@ -128,10 +128,13 @@
     def next_row(j):
         row = lax.rem(y + NY - j, NY)
         drain(xg.at[:, z, c, row], y_recv.at[j - 1])
+        if j != 2:
+            half = xg.at[j // 2, z, c, row]
+            remote(half, half, y_send, y_recv.at[1], at(z, lax.rem(y + j, NY), c), n).start()
         first_row(row)
 
     own = xg.at[:, z, c, y]
-    for j in (1, 3, 2):
+    for j in (1, 3):
         remote(own, own, y_send, y_recv.at[j - 1], at(z, lax.rem(y + j, NY), c), n).start()
     first_row(y)
     load_in.wait()

time: 80.8 us -> 81.6 us (level)
  no operation moved by 1% of the time
where the time goes in v8:
time: 81.6 us; the launch traced here: 81.5 us
  Pallas kernels  80.8 us (99%)
    pallas_call x1, Pallas kernels, local(): pl.pallas_call(kernel, out_shape=(jax.ShapeDtypeStruct((ROWS, FEAT), F32)...  79.3 us

profile of v8, /device:TPU:1, one launch (start us, length us, event | category | flops | bytes accessed | tf_op | source)
XLA Modules:
  0.0 81.5 jit_solution(10575484202780675616)
XLA Ops:
  0.6 79.3 %shard_map.92 = (f32[8,768]{1,0:T(8,128)S(1)}, f32[768,384]{1,0:T(8,128)S(1)}, f32[384,768]{1,0:T(8,128)S(1)}, f32[1,384]{1,0:T(1,128)S(1)}, f32[1,768]{1,0:T(1,128)S(1)}, /*index=5*/f32[8,128]{1,0:T(8,128)S(1)}) custom-call(f32[8,768]{1,0:T(8,128)} %x_ref.1, f32[8,768]{1,0:T(8,128)} %g_ref.1, f32[768,384]{1,0:T(8,128)} %w_in_ref.1, f32[384]{0:T(512)} %b_ref.1, ...), custom_call_target="tpu_custom_call" | custom-call | tf_op jit(solution)/shard_map/pallas_call | solution.py:417
  79.9 1.5 %shard_map.93 = (f32[8,768]{1,0:T(8,128)}, f32[768,384]{1,0:T(8,128)}, f32[384,768]{1,0:T(8,128)}, f32[384]{0:T(512)}, f32[768]{0:T(1024)}) custom-call(f32[8,768]{1,0:T(8,128)S(1)} %get-tuple-element.11.grad_in_ref, f32[768,384]{1,0:T(8,128)S(1)} %get-tuple-element.12.raw_in_ref, f32[384,768]{1,0:T(8,128)S(1)} %get-tuple-element.13.raw_out_ref, ...), custom_call_target="tpu_custom_call" | custom-call | tf_op jit(solution)/shard_map/pallas_call | solution.py:474

commit v9 on v7

--- a/solution.py
+++ b/solution.py
@@ -21,7 +21,6 @@
 PLACES = ((1152, 128, 0), (0, 256, 0), (0, 256, 128), (768, 128, 0), (1152, 128, 64))
 ROUNDS = ((0, 768), (768, 384), (1152, 384))
 SUM_COLUMNS = 1536
-FIRST_Y = 7
 STEPS = (
     "x0h1a11001x1h230a211h30240x231a3h41203a460x3b0410470",
     "x4133261b114337142346243b2v0v1724463b3w0w16473b4u0u1",
@@ -75,12 +74,12 @@
 def kernel(
     x_ref, g_ref, w_in_ref, b_ref, w_out_ref,
     grad_in_ref, raw_in_ref, raw_out_ref, bias_in_ref, bias_out_ref, factor_ref,
-    xg, part, relay, near, ag, gi, gi_core, gi_z, gi_y, gi_y_first, gi_z_last, sums,
+    xg, part, relay, near, ag, gi, gi_core, gi_z, gi_y, sums,
     w_in_f, w_out_f, w_in_h, w_in_l, w_out_h, w_out_l, w_back_h, w_back_l,
     x_across, g_along, p_along, a_across, bias, b_here,
     load_sem, y_send, y_recv, z_send, z_recv, c_send, c_recv,
     f_send, f_recv, n_send, n_recv, a_send, a_one_recv, a_far_recv,
-    gc_send, gc_recv, gz_send, gz_recv, gy_send, gy_recv, gyf_send, gyf_recv, gzl_send, gzl_recv,
+    gc_send, gc_recv, gz_send, gz_recv, gy_send, gy_recv,
     s_send, s_recv,
 ):
     wide = lax.axis_index("wide")
@@ -253,28 +252,10 @@
         drain(gi_core.at[pl.ds(first, count)], gc_recv.at[group])
         for k in range(first, first + count):
             gi[k, c] += gi_core[k]
-            if 0 < k < FIRST_Y:
+            if k > 0:
                 remote(
                     gi.at[k, c], gi_z.at[k - 1], gz_send, gz_recv, at(block_of(k), y, c), n
                 ).start()
-        if first >= FIRST_Y:
-            for j in (2, 1, 3):
-                to = lax.rem(y + j, NY)
-                remote(
-                    gi.at[pl.ds(first, count), c, to],
-                    gi_y_first.at[j - 1, pl.ds(first - FIRST_Y, count)],
-                    gyf_send, gyf_recv, at(z, to, c), n,
-                ).start()
-
-    def to_owner(group):
-        first, count = GROUPS[group]
-        drain(gi_y_first, gyf_recv)
-        for k in range(first, first + count):
-            i = k - FIRST_Y
-            gi[k, c, y] += gi_y_first[0, i] + (gi_y_first[1, i] + gi_y_first[2, i])
-            remote(
-                gi.at[k, c, y], gi_z_last.at[i], gzl_send, gzl_recv, at(block_of(k), y, c), n
-            ).start()
 
     def to_vreg(squares):
         rows, columns = squares.shape
@@ -341,10 +322,9 @@
     share(1, plane, total, [
         (z * NY * NC + lax.rem(plane + j, NY * NC), n) for j in range(1, 8)
     ])
-    to_owner(4)
     drain(gi_z, gz_recv)
     own_sum = gi[0, c]
-    for j in range(FIRST_Y - 1):
+    for j in range(NZ - 1):
         own_sum = own_sum + gi_z[j]
     gi[0, c] = own_sum
     for j in (2, 1, 3):
@@ -357,8 +337,7 @@
         (lax.rem(z + j, NZ) * NY * NC + plane, n) for j in range(1, 8)
     ])
     drain(gi_y, gy_recv)
-    drain(gi_z_last, gzl_recv)
-    grad_in_ref[...] = ((gi[0, c, y] + gi_y[0]) + (gi_y[1] + gi_y[2])) + gi_z_last[0]
+    grad_in_ref[...] = (gi[0, c, y] + gi_y[0]) + (gi_y[1] + gi_y[2])
     drain(xg.at[:, z, c, pl.ds(0, 3)], y_send)
     drain(xg.at[:, pl.ds(0, 7), 0], z_send)
     drain(xg.at[:, :, 0], c_send)
@@ -368,8 +347,6 @@
     drain(gi_core, gc_send)
     drain(gi_z, gz_send)
     drain(gi_y, gy_send)
-    drain(gi_y_first, gyf_send)
-    drain(gi_z_last, gzl_send)
     total = jnp.sum(collect(2), keepdims=True)
     factor = jnp.minimum(1.0, math.sqrt(1.0 * D * FF * TOKENS) / (jnp.sqrt(total) + 1e-06))
     factor_ref[...] = jnp.broadcast_to(factor, factor_ref.shape)
@@ -431,10 +408,8 @@
             pltpu.VMEM((NN, NZ, 2, ROWS, HID), F32),
             pltpu.VMEM((NZ, NC, NY, ROWS, FEAT), F32),
             pltpu.VMEM((NZ, NY, ROWS, FEAT), F32),
-            pltpu.VMEM((FIRST_Y - 1, NY, ROWS, FEAT), F32),
+            pltpu.VMEM((NZ - 1, NY, ROWS, FEAT), F32),
             pltpu.VMEM((NY - 1, ROWS, FEAT), F32),
-            pltpu.VMEM((NY - 1, NZ - FIRST_Y, ROWS, FEAT), F32),
-            pltpu.VMEM((NZ - FIRST_Y, ROWS, FEAT), F32),
             pltpu.VMEM((3, 8, 8, 128), F32),
             pltpu.VMEM((FEAT, HID), F32),
             pltpu.VMEM((HID, FEAT), F32),
@@ -458,8 +433,6 @@
             dma, dma((5,)),
             dma, dma((5,)), dma((5,)),
             dma, dma((5,)),
-            dma, dma,
-            dma, dma,
             dma, dma,
             dma, dma,
             dma, dma((3,)),

time: 80.8 us -> 85.1 us (1.053)
  Pallas kernels: 80 us -> 84.3 us
    pallas_call x1, Pallas kernels: 78.5 us -> 82.8 us  [local(): pl.pallas_call(kernel, out_shape=(jax.ShapeDtypeStruct((ROWS, FEAT), F32)...]
where the time goes in v9:
time: 85.1 us; the launch traced here: 85 us
  Pallas kernels  84.3 us (99%)
    pallas_call x1, Pallas kernels, local(): pl.pallas_call(kernel, out_shape=(jax.ShapeDtypeStruct((ROWS, FEAT), F32)...  82.8 us

profile of v9, /device:TPU:1, one launch (start us, length us, event | category | flops | bytes accessed | tf_op | source)
XLA Modules:
  0.0 85.0 jit_solution(9767065107353557070)
XLA Ops:
  0.6 82.8 %shard_map.92 = (f32[8,768]{1,0:T(8,128)S(1)}, f32[768,384]{1,0:T(8,128)S(1)}, f32[384,768]{1,0:T(8,128)S(1)}, f32[1,384]{1,0:T(1,128)S(1)}, f32[1,768]{1,0:T(1,128)S(1)}, /*index=5*/f32[8,128]{1,0:T(8,128)S(1)}) custom-call(f32[8,768]{1,0:T(8,128)} %x_ref.1, f32[8,768]{1,0:T(8,128)} %g_ref.1, f32[768,384]{1,0:T(8,128)} %w_in_ref.1, f32[384]{0:T(512)} %b_ref.1, ...), custom_call_target="tpu_custom_call" | custom-call | tf_op jit(solution)/shard_map/pallas_call | solution.py:391
  83.4 1.5 %shard_map.93 = (f32[8,768]{1,0:T(8,128)}, f32[768,384]{1,0:T(8,128)}, f32[384,768]{1,0:T(8,128)}, f32[384]{0:T(512)}, f32[768]{0:T(1024)}) custom-call(f32[8,768]{1,0:T(8,128)S(1)} %get-tuple-element.11.grad_in_ref, f32[768,384]{1,0:T(8,128)S(1)} %get-tuple-element.12.raw_in_ref, f32[384,768]{1,0:T(8,128)S(1)} %get-tuple-element.13.raw_out_ref, ...), custom_call_target="tpu_custom_call" | custom-call | tf_op jit(solution)/shard_map/pallas_call | solution.py:444
